TPU v7x, 512 devices: a whole 4x4x16 slice. The times are simulated.
512 devices in a mesh: group: 64 (over z, y), local: 8 (over x, core).
Axes of the slice: x: 4, y: 4, z: 16, core: 2. Of those that a mesh axis runs over, the one named last changes fastest.
Arguments:
- tokens: bfloat16 [16384, 2560], P(('group', 'local')), may hold values from -6 to 6
- chosen_groups: int32 [16384, 3], P(('group', 'local')), may hold values from 0 to 15, as said below
- local_picks: int32 [16384, 6], P(('group', 'local')), may hold values from 0 to 7, as said below
- gate_probs: float32 [16384, 6], P(('group', 'local')), may hold values from 0.02 to 0.5
- w_gate: bfloat16 [8, 16384, 2560], P('local', 'group'), may hold values from -0.125 to 0.125
- w_up: bfloat16 [8, 16384, 2560], P('local', 'group'), may hold values from -0.125 to 0.125
- w_down: bfloat16 [8, 16384, 2560], P('local', 'group'), may hold values from -0.1875 to 0.1875
Outputs:
- mixed: bfloat16 [16384, 2560], P(('group', 'local'))
Inputs may be any that keep to these rules, and one draw needn't show every extreme that they name: `chosen_groups`: each token's 3 entries are different. Among the 32 tokens of one device (aligned blocks of rows), no routing group is chosen by more than 8 tokens, and some group by exactly 8 in every block. `local_picks`: entries 2 j and 2 j + 1 are different. Among the tokens of one device, no expert (chosen group, index) is used more than 2 times, and some expert exactly 2 times in every block.
All inputs are finite; a program needn't handle non-finite values.
Results may differ from a plain program's by a relative error of at most 0.0058.
Values may be sent and summed in bfloat16 or wider, within the bound.
No kernel may reach another device: no remote copies, remote signals or barrier semaphores. Data moves between devices by JAX's collectives and lax.ppermute only.
A program may use at most 64 MiB of HBM per device.

v0:
```python
import jax
import jax.numpy as jnp
from jax import lax
from jax.sharding import PartitionSpec as P

TOP = 6
TOP_GROUPS = 3
SHARDS = 4


def running_rank(labels, width):
    hits = (labels[:, None] == jnp.arange(width, dtype=jnp.int32)[None, :]).astype(jnp.int32)
    before = jnp.cumsum(hits, axis=0) - hits
    return jnp.sum(before * hits, axis=1)


def expert_rows(block, w_gate, w_up, w_down):
    shape = block.shape
    rows = block.reshape(-1, shape[-1])
    contract = (((1,), (1,)), ((), ()))
    gate_part = lax.dot_general(rows, w_gate[0], contract, preferred_element_type=jnp.float32)
    up_part = lax.dot_general(rows, w_up[0], contract, preferred_element_type=jnp.float32)
    hidden = (jax.nn.silu(gate_part) * up_part).astype(jnp.bfloat16)
    result = jnp.dot(hidden, w_down[0], preferred_element_type=jnp.float32).astype(jnp.bfloat16)
    return result.reshape(shape)


def pack_rows(tokens, slots, n_slots, per_token):
    tok_count, width = tokens.shape
    owners = jnp.repeat(jnp.arange(tok_count, dtype=jnp.int32), per_token)
    source = jnp.full((n_slots,), tok_count, jnp.int32).at[slots.reshape(-1)].set(owners)
    padded = jnp.concatenate([tokens, jnp.zeros((1, width), tokens.dtype)], axis=0)
    return padded[source]


def on_device(tokens, chosen_groups, local_picks, gate_probs, w_gate, w_up, w_down):
    n_group = lax.axis_size("group")
    n_local = lax.axis_size("local")
    n_rg = n_group // SHARDS
    tok_count, width = tokens.shape
    c_one = TOP_GROUPS * tok_count // n_rg + 2
    c_exp = (2 * c_one + n_local - 1) // n_local
    pick_group = jnp.repeat(chosen_groups, 2, axis=1)
    pick_rank = running_rank(
        (pick_group * n_local + local_picks).reshape(-1), n_rg * n_local
    ).reshape(tok_count, TOP)
    slots = (local_picks * n_rg + pick_group) * c_exp + pick_rank
    n_slots = n_local * n_rg * c_exp
    packed = pack_rows(tokens, slots, n_slots, TOP).reshape(n_local, n_rg, 1, c_exp, width)
    arrived = lax.all_to_all(packed, "local", split_axis=0, concat_axis=2, tiled=True)
    copies = jnp.broadcast_to(
        arrived.reshape(n_rg, 1, n_local, c_exp, width), (n_rg, SHARDS, n_local, c_exp, width)
    )
    copies = copies.reshape(n_group, n_local, c_exp, width)
    outputs = expert_rows(
        lax.all_to_all(copies, "group", split_axis=0, concat_axis=0, tiled=True),
        w_gate,
        w_up,
        w_down,
    )
    returned = lax.all_to_all(outputs, "group", split_axis=0, concat_axis=0, tiled=True)
    summed = jnp.sum(
        returned.astype(jnp.float32).reshape(n_rg, SHARDS, n_local, c_exp, width), axis=1
    )
    back = lax.all_to_all(summed, "local", split_axis=1, concat_axis=1, tiled=True)
    flat = back.reshape(-1, width)
    index = (pick_group * n_local + local_picks) * c_exp + pick_rank
    picked = flat[index]
    result = jnp.sum(picked * gate_probs[:, :, None], axis=1)
    return result.astype(jnp.bfloat16)


def solution(mesh):
    return jax.shard_map(
        on_device,
        mesh=mesh,
        in_specs=(
            P(("group", "local"), None),
            P(("group", "local"), None),
            P(("group", "local"), None),
            P(("group", "local"), None),
            P("local", "group", None),
            P("local", "group", None),
            P("local", "group", None),
        ),
        out_specs=P(("group", "local"), None),
        check_vma=False,
    )
```

profile of v0, /device:TPU:1, one launch (start us, length us, event | category | flops | bytes accessed | tf_op | source)
XLA Modules:
  0.0 633.6 jit_solution(414725751147036178)
XLA Ops:
  0.0 0.0 copy-start
  0.0 0.8 broadcast_in_dim.27
  0.8 0.7 multiply_add_fusion
  1.5 0.1 copy.37
  1.6 0.1 eq.22
  1.7 0.1 iota_compare_fusion
  1.8 0.1 fusion.15
  2.0 0.2 fusion.18
  2.2 0.1 reshape.80
  2.3 0.1 copy.40
  2.4 0.7 compare_select_fusion
  3.1 0.1 copy.41
  3.2 0.1 reshape.81
  3.3 0.1 reshape.113
  3.4 1.2 scatter_custom_fusion
  4.7 0.9 concatenate.3
  5.6 1.4 gather_fusion
  7.1 1.4 reshape.83
  8.4 28.3 %all_to_all.30 = bf16[8,16,1,2,2560]{4,3,1,2,0:T(2,128)(2,1)S(1)} all-to-all(bf16[8,16,1,2,2560]{4,3,1,2,0:T(2,128)(2,1)} %bitcast.38), channel_id=1, replica_groups=mesh['group'=64,'local'=8] {'local'}, dimensions={0} | all-to-all | bytes 2621440 | tf_op jit(solution)/shard_map/all_to_all | solution.py:50
  36.7 1.2 copy.43
  37.9 4.9 broadcast_in_dim.31
  42.8 244.7 %all_to_all.31 = bf16[64,8,2,2560]{3,2,1,0:T(2,128)(2,1)} all-to-all(bf16[64,8,2,2560]{3,2,1,0:T(2,128)(2,1)S(1)} %bitcast.37), channel_id=1, replica_groups=mesh['group'=64,'local'=8] {'group'}, dimensions={0} | all-to-all | bytes 10485760 | tf_op jit(solution)/shard_map/all_to_all | solution.py:56
  287.5 0.0 copy-start.2
  287.5 11.8 %reshape.85 = bf16[1024,2560]{1,0:T(8,128)(2,1)} reshape(bf16[64,8,2,2560]{3,2,1,0:T(2,128)(2,1)} %all_to_all.31) | data formatting | bytes 10485760 | tf_op jit(solution)/shard_map/reshape | solution.py:19
  299.2 0.0 copy-done.2
  299.2 5.0 fusion.2
  304.2 0.0 copy-done
  304.3 10.9 %convolution_convert_fusion = bf16[1024,2560]{1,0:T(8,128)(2,1)} fusion(bf16[1,256,2560]{2,1,0:T(8,128)(2,1)S(1)} %copy-done, bf16[1024,2560]{1,0:T(8,128)(2,1)} %reshape.85, bf16[1,256,2560]{2,1,0:T(8,128)(2,1)} %param.12, f32[1024,256]{1,0:T(8,128)} %fusion.2), kind=kOutput, calls=%fused_computation.4 | convolution fusion | flops 2688548864 | bytes 14155776 | tf_op jit(solution)/shard_map/dot_general | solution.py:24
  315.2 11.2 %reshape.86 = bf16[64,8,2,2560]{3,2,1,0:T(2,128)(2,1)} reshape(bf16[1024,2560]{1,0:T(8,128)(2,1)} %convolution_convert_fusion) | data formatting | bytes 10485760 | tf_op jit(solution)/shard_map/reshape | solution.py:25
  326.4 240.8 %all_to_all.32 = bf16[64,8,2,2560]{3,2,1,0:T(2,128)(2,1)S(1)} all-to-all(bf16[64,8,2,2560]{3,2,1,0:T(2,128)(2,1)} %reshape.86), channel_id=1, replica_groups=mesh['group'=64,'local'=8] {'group'}, dimensions={0} | all-to-all | bytes 10485760 | tf_op jit(solution)/shard_map/all_to_all | solution.py:61
  567.2 6.5 %convert_reduce_fusion = f32[16,8,2,2560]{3,2,1,0:T(2,128)S(1)} fusion(bf16[64,8,2,2560]{3,2,1,0:T(2,128)(2,1)S(1)} %all_to_all.32), kind=kLoop, calls=%fused_computation.3 | loop fusion | flops 4587520 | bytes 7864320 | tf_op jit(solution)/shard_map/reduce_sum | solution.py:62
  573.7 1.7 copy.44
  575.4 0.0 copy-start.1
  575.4 9.1 %all-to-all-start.3 = ((f32[16,8,2,2560]{3,2,0,1:T(2,128)}), f32[16,8,2,2560]{3,2,0,1:T(2,128)}, u32[]{:S(2)}, u32[]{:S(2)}) async-start(f32[16,8,2,2560]{3,2,0,1:T(2,128)} %copy.44), calls=%async_computation.3 | async-start | bytes 5242880 | tf_op jit(solution)/shard_map/all_to_all | solution.py:65
  584.5 0.1 copy.47
  584.6 0.1 reshape.103
  584.7 0.0 copy-done.1
  584.7 0.1 copy.48
  584.8 31.8 %all-to-all-done.3 = f32[16,8,2,2560]{3,2,0,1:T(2,128)} async-done(((f32[16,8,2,2560]{3,2,0,1:T(2,128)}), f32[16,8,2,2560]{3,2,0,1:T(2,128)}, u32[]{:S(2)}, u32[]{:S(2)}) %all-to-all-start.3) | async-done | bytes 2621472 | tf_op jit(solution)/shard_map/all_to_all | solution.py:65
  616.6 3.5 copy.45
  620.1 4.5 reshape.89
  624.6 4.0 gather_fusion.1
  628.6 1.7 reshape.102
  630.2 3.3 multiply_reduce_fusion
  (13 shorter events, 0.1 us)
Async XLA Ops:
  0.0 304.3 %copy-start = (bf16[1,256,2560]{2,1,0:T(8,128)(2,1)S(1)}, bf16[1,256,2560]{2,1,0:T(8,128)(2,1)}, u32[]{:S(2)}) copy-start(bf16[1,256,2560]{2,1,0:T(8,128)(2,1)} %param.13) | copy-start | bytes 3932164
  287.5 11.8 %copy-start.2 = (bf16[1,256,2560]{2,1,0:T(8,128)(2,1)S(1)}, bf16[1,256,2560]{2,1,0:T(8,128)(2,1)}, u32[]{:S(2)}) copy-start(bf16[1,256,2560]{2,1,0:T(8,128)(2,1)} %param.11) | copy-start | bytes 3932164
  575.4 9.3 %copy-start.1 = (f32[32,6]{0,1:T(8,128)S(1)}, f32[32,6]{0,1:T(8,128)}, u32[]{:S(2)}) copy-start(f32[32,6]{0,1:T(8,128)} %param.10) | copy-start | bytes 2308
  575.4 41.2 %all-to-all-start.3 = ((f32[16,8,2,2560]{3,2,0,1:T(2,128)}), f32[16,8,2,2560]{3,2,0,1:T(2,128)}, u32[]{:S(2)}, u32[]{:S(2)}) async-start(f32[16,8,2,2560]{3,2,0,1:T(2,128)} %copy.44), calls=%async_computation.3 | async-start | bytes 5242880 | tf_op jit(solution)/shard_map/all_to_all | solution.py:65
where the time goes:
time: 635 us; the launch traced here: 634 us
  blocking collectives  514 us (81%)
  local copies, waits for them, and re-layouts  51.2 us (8%)
  waiting for transfers between devices  31.8 us (5%)
  matrix products  15.9 us (3%)
  other arithmetic  11.7 us (2%)
  starting transfers between devices  9.13 us (1%)
    all_to_all x1, blocking collectives, on_device(): lax.all_to_all(copies, 'group', split_axis=0, concat_axis=0, tiled=True)  245 us
    all_to_all x1, blocking collectives, on_device(): lax.all_to_all(outputs, 'group', split_axis=0, concat_axis=0, tiled=True)  241 us
    all_to_all x1, waiting for transfers between devices, on_device(): lax.all_to_all(summed, 'local', split_axis=1, concat_axis=1, tiled=True)  31.8 us
    all_to_all x1, blocking collectives, on_device(): lax.all_to_all(packed, 'local', split_axis=0, concat_axis=2, tiled=True)  28.3 us
  transfers between devices with their start and end apart: 1, of which 1 were waited for; matrix products, arithmetic and copies ran while one was open for 0% of the time, Pallas kernels for 0%

commit v1 on v0

v1 whole, which is shorter than its diff:
```python
import jax
import jax.numpy as jnp
from jax import lax
from jax.sharding import Mesh, PartitionSpec as P

TOP_GROUPS = 3
N_RG = 16
SHARDS = 4
LEXP = 8
CE = 2
CG = 8
META = 128
BF = jnp.bfloat16
F32 = jnp.float32


def strict_before(n):
    return (jnp.arange(n)[:, None] > jnp.arange(n)[None, :]).astype(F32)


def pack(tokens, chosen_groups, local_picks, gate_probs):
    tok, width = tokens.shape
    picks = local_picks.reshape(tok, TOP_GROUPS, 2).astype(F32)
    gates = gate_probs.reshape(tok, TOP_GROUPS, 2)
    here = (chosen_groups[:, :, None] == jnp.arange(N_RG, dtype=jnp.int32)).astype(F32)
    member = jnp.sum(here, axis=1)
    rank = jnp.dot(strict_before(tok), member, precision=lax.Precision.HIGHEST)
    slot = (rank.T[:, None, :] == jnp.arange(CG, dtype=F32)[None, :, None]) & (
        member.T[:, None, :] > 0
    )
    slot = slot.astype(F32)
    values = jnp.concatenate([picks + 1.0, gates], axis=2)
    by_group = jnp.sum(here[:, :, :, None] * values[:, :, None, :], axis=1)
    meta = jnp.sum(slot[:, :, :, None] * by_group.transpose(1, 0, 2)[:, None, :, :], axis=2)
    meta = meta.reshape(N_RG * CG, 4)
    gate = meta[:, 2:]
    high = gate.astype(BF)
    low = (gate - high.astype(F32)).astype(BF)
    least = (gate - high.astype(F32) - low.astype(F32)).astype(BF)
    cols = jnp.concatenate([meta[:, :2].astype(BF), high, low, least], axis=1)
    cols = jnp.pad(cols, ((0, 0), (0, META - cols.shape[1])))
    slot = slot.reshape(N_RG * CG, tok).astype(BF)
    rows = jnp.dot(slot, tokens, preferred_element_type=F32).astype(BF)
    return jnp.concatenate([rows, cols], axis=1), slot


def spread(cols):
    info = cols.astype(F32).reshape(N_RG, CG, -1)
    picks = info[:, :, :2]
    gates = info[:, :, 2:4] + info[:, :, 4:6] + info[:, :, 6:8]
    lanes = jnp.arange(LEXP, dtype=F32) + 1.0
    match = (picks[:, :, :, None] == lanes).astype(F32)
    hit = jnp.sum(match, axis=2)
    weight = jnp.sum(match * gates[:, :, :, None], axis=2)
    rank = jnp.einsum(
        "rs,zsl->zrl", strict_before(CG), hit, precision=lax.Precision.HIGHEST
    )
    place = (rank[:, :, :, None] == jnp.arange(CE, dtype=F32)) & (hit[:, :, :, None] > 0)
    place = place.astype(F32)
    same = jnp.eye(N_RG, dtype=F32)
    chosen = (
        place.transpose(2, 0, 3, 1)[:, :, :, None, :] * same[None, :, None, :, None]
    ).reshape(LEXP * N_RG * CE, N_RG * CG)
    scaled = chosen * weight.transpose(2, 0, 1).reshape(LEXP, 1, N_RG * CG).repeat(
        N_RG * CE, axis=1
    ).reshape(LEXP * N_RG * CE, N_RG * CG)
    return chosen.astype(BF), scaled


def experts(rows, w_gate, w_up, w_down):
    contract = (((1,), (1,)), ((), ()))
    gate_part = lax.dot_general(rows, w_gate, contract, preferred_element_type=F32)
    up_part = lax.dot_general(rows, w_up, contract, preferred_element_type=F32)
    hidden = (jax.nn.silu(gate_part) * up_part).astype(BF)
    return jnp.dot(hidden, w_down, preferred_element_type=F32).astype(BF)


def on_device(tokens, chosen_groups, local_picks, gate_probs, w_gate, w_up, w_down):
    tok, width = tokens.shape
    packed, slot = pack(tokens, chosen_groups, local_picks, gate_probs)
    arrived = lax.all_to_all(packed.reshape(N_RG, CG, -1), "z", 0, 0, tiled=True)
    arrived = arrived.reshape(N_RG * CG, -1)
    chosen, scaled = spread(arrived[:, width : width + 8])
    rows = jnp.dot(chosen, arrived[:, :width], preferred_element_type=F32).astype(BF)
    rows = jnp.broadcast_to(rows.reshape(1, LEXP, -1, width), (SHARDS, LEXP, N_RG * CE, width))
    rows = rows.reshape(SHARDS * LEXP, N_RG * CE, width)
    rows = lax.all_to_all(rows, ("y", "x", "c"), 0, 0, tiled=True)
    outs = experts(rows.reshape(-1, width), w_gate[0], w_up[0], w_down[0])
    outs = outs.reshape(SHARDS * LEXP, N_RG * CE, width)
    outs = lax.all_to_all(outs, ("y", "x", "c"), 0, 0, tiled=True)
    outs = outs.reshape(-1, width)
    high = scaled.astype(BF)
    low = (scaled - high.astype(F32)).astype(BF)
    contract = (((0,), (0,)), ((), ()))
    high = jnp.tile(high, (SHARDS, 1))
    low = jnp.tile(low, (SHARDS, 1))
    both = lax.dot_general(
        jnp.concatenate([high, low], axis=1), outs, contract, preferred_element_type=F32
    )
    mixed = (both[: N_RG * CG] + both[N_RG * CG :]).astype(BF)
    home = lax.all_to_all(mixed.reshape(N_RG, CG, width), "z", 0, 0, tiled=True)
    home = home.reshape(N_RG * CG, width)
    return lax.dot_general(slot, home, contract, preferred_element_type=F32).astype(BF)


def solution(mesh):
    grid = Mesh(mesh.devices.reshape(N_RG, SHARDS, 4, 2), ("z", "y", "x", "c"))
    every = ("z", "y", "x", "c")
    weights = P(("x", "c"), ("z", "y"), None)
    return jax.shard_map(
        on_device,
        mesh=grid,
        in_specs=(P(every, None),) * 4 + (weights,) * 3,
        out_specs=P(every, None),
        check_vma=False,
    )
```

time: 635 us -> 264 us (0.42)
  the two profiles are of different devices: /device:TPU:1 before, /device:TPU:42 now
where the time goes in v1:
time: 264 us; the launch traced here: 263 us
  blocking collectives  110 us (42%)
  waiting for transfers between devices  98.3 us (37%)
  starting transfers between devices  23.4 us (9%)
  matrix products  21.2 us (8%)
  local copies, waits for them, and re-layouts  5.79 us (2%)
  other arithmetic  4.56 us (2%)
    all_to_all x1, blocking collectives, on_device(): rows = lax.all_to_all(rows, ('y', 'x', 'c'), 0, 0, tiled=True)  66.4 us
    all_to_all x1, waiting for transfers between devices, on_device(): outs = lax.all_to_all(outs, ('y', 'x', 'c'), 0, 0, tiled=True)  63.2 us
    all_to_all x1, blocking collectives, on_device(): home = lax.all_to_all(mixed.reshape(N_RG, CG, width), 'z', 0, 0, tiled=True)  43.6 us
    all_to_all x1, waiting for transfers between devices, on_device(): lax.all_to_all(packed.reshape(N_RG, CG, -1), 'z', 0, 0, tiled=True)  35.2 us
    all_to_all x1, starting transfers between devices, on_device(): lax.all_to_all(packed.reshape(N_RG, CG, -1), 'z', 0, 0, tiled=True)  15.2 us
    dot_general x1, matrix products, experts(): return jnp.dot(hidden, w_down, preferred_element_type=F32).astype(BF)  10.6 us
    all_to_all x1, starting transfers between devices, on_device(): outs = lax.all_to_all(outs, ('y', 'x', 'c'), 0, 0, tiled=True)  8.21 us
  transfers between devices with their start and end apart: 2, of which 2 were waited for; matrix products, arithmetic and copies ran while one was open for 0% of the time, Pallas kernels for 0%

profile of v1, /device:TPU:42, one launch (start us, length us, event | category | flops | bytes accessed | tf_op | source)
XLA Modules:
  0.0 263.5 jit_solution(8147081042034942460)
XLA Ops:
  0.0 0.0 copy-start
  0.0 0.8 fusion.41
  0.8 0.1 fusion.39
  0.9 0.7 fusion.38
  1.6 0.7 convert_add_fusion
  2.3 0.7 reshape.136
  3.1 0.2 multiply_reduce_fusion
  3.3 0.1 reshape.137
  3.4 0.1 copy.59
  3.6 0.1 eq.94
  3.7 1.3 convolution_convert_fusion.2
  5.0 0.9 fusion.18
  5.9 15.2 %all-to-all-start = ((bf16[16,8,2688]{2,1,0:T(8,128)(2,1)}), bf16[16,8,2688]{2,1,0:T(8,128)(2,1)S(1)}, u32[]{:S(2)}, u32[]{:S(2)}) async-start(bf16[16,8,2688]{2,1,0:T(8,128)(2,1)} %fusion.18), calls=%async_computation | async-start | bytes 1376256 | tf_op jit(solution)/shard_map/all_to_all | solution.py:81
  21.1 35.2 %all-to-all-done = bf16[16,8,2688]{2,1,0:T(8,128)(2,1)S(1)} async-done(((bf16[16,8,2688]{2,1,0:T(8,128)(2,1)}), bf16[16,8,2688]{2,1,0:T(8,128)(2,1)S(1)}, u32[]{:S(2)}, u32[]{:S(2)}) %all-to-all-start) | async-done | bytes 688160 | tf_op jit(solution)/shard_map/all_to_all | solution.py:81
  56.2 0.0 copy-start.2
  56.2 0.1 copy.67
  56.3 0.1 reshape.149
  56.4 0.1 copy.61
  56.5 0.1 copy.65
  56.6 0.7 fusion.28
  57.3 0.1 convolution_bitcast_fusion.1
  57.4 0.1 copy.63
  57.5 0.1 copy.64
  57.6 0.0 copy-done.2
  57.7 0.1 and_convert_fusion
  57.8 0.2 broadcast_multiply_fusion
  58.0 1.0 mul.84
  59.0 1.6 convolution_convert_fusion.1
  60.6 0.6 broadcast_in_dim.8
  61.2 0.0 copy-start.4
  61.2 66.4 %all_to_all.20 = bf16[32,32,2560]{2,1,0:T(8,128)(2,1)S(1)} all-to-all(bf16[32,32,2560]{2,1,0:T(8,128)(2,1)S(1)} %bitcast.74), channel_id=1, replica_groups=mesh['z'=16,'y'=4,'x'=4,'c'=2] {'y','x','c'}, dimensions={0} | all-to-all | bytes 10485760 | tf_op jit(solution)/shard_map/all_to_all | solution.py:87
  127.6 0.0 copy-start.1
  127.6 2.3 copy-done.1
  129.9 0.0 copy-done.4
  129.9 0.0 copy-start.5
  129.9 2.5 fusion.5
  132.5 0.0 copy-done
  132.5 0.0 copy-done.5
  132.5 10.6 %convolution_convert_fusion = bf16[1024,2560]{1,0:T(8,128)(2,1)} fusion(bf16[1,256,2560]{2,1,0:T(8,128)(2,1)S(1)} %copy-done, bf16[1024,2560]{1,0:T(8,128)(2,1)} %bitcast.77, bf16[1,256,2560]{2,1,0:T(8,128)(2,1)S(1)} %copy-done.5, f32[1024,256]{1,0:T(8,128)} %fusion.5), kind=kOutput, calls=%fused_computation | convolution fusion | flops 2688548864 | bytes 14155776 | tf_op jit(solution)/shard_map/dot_general | solution.py:75
  143.0 0.0 copy-start.3
  143.0 8.2 %all-to-all-start.2 = ((bf16[32,32,2560]{2,1,0:T(8,128)(2,1)}), bf16[32,32,2560]{2,1,0:T(8,128)(2,1)}, u32[]{:S(2)}, u32[]{:S(2)}) async-start(bf16[32,32,2560]{2,1,0:T(8,128)(2,1)} %bitcast.75), calls=%async_computation.2 | async-start | bytes 10485760 | tf_op jit(solution)/shard_map/all_to_all | solution.py:90
  151.2 0.0 copy-done.3
  151.3 0.1 copy.66
  151.3 0.1 reshape.142
  151.5 63.2 %all-to-all-done.2 = bf16[32,32,2560]{2,1,0:T(8,128)(2,1)} async-done(((bf16[32,32,2560]{2,1,0:T(8,128)(2,1)}), bf16[32,32,2560]{2,1,0:T(8,128)(2,1)}, u32[]{:S(2)}, u32[]{:S(2)}) %all-to-all-start.2) | async-done | bytes 5242912 | tf_op jit(solution)/shard_map/all_to_all | solution.py:90
  214.7 4.0 %fusion.21 = f32[256,2560]{1,0:T(8,128)S(1)} fusion(bf16[1024,2560]{1,0:T(8,128)(2,1)} %bitcast.20, bf16[1024,128]{1,0:T(8,128)(2,1)S(1)} %bitcast.82, bf16[1024,128]{1,0:T(8,128)(2,1)S(1)} %bitcast.81), kind=kOutput, calls=%fused_computation.26 | convolution fusion | flops 1343225856 | bytes 8388608 | tf_op jit(solution)/shard_map/dot_general | solution.py:97
  218.8 0.1 fusion.19
  218.9 43.6 %all_to_all.21 = bf16[16,8,2560]{2,1,0:T(8,128)(2,1)S(1)} all-to-all(bf16[16,8,2560]{2,1,0:T(8,128)(2,1)S(1)} %fusion.19), channel_id=1, replica_groups=mesh['z'=16,'y'=4,'x'=4,'c'=2] {'z'}, dimensions={0} | all-to-all | bytes 1310720 | tf_op jit(solution)/shard_map/all_to_all | solution.py:101
  262.5 0.9 fusion
  (20 shorter events, 0.2 us)
Async XLA Ops:
  0.0 132.5 %copy-start = (bf16[1,256,2560]{2,1,0:T(8,128)(2,1)S(1)}, bf16[1,256,2560]{2,1,0:T(8,128)(2,1)}, u32[]{:S(2)}) copy-start(bf16[1,256,2560]{2,1,0:T(8,128)(2,1)} %param.13) | copy-start | bytes 3932164
  5.9 50.4 %all-to-all-start = ((bf16[16,8,2688]{2,1,0:T(8,128)(2,1)}), bf16[16,8,2688]{2,1,0:T(8,128)(2,1)S(1)}, u32[]{:S(2)}, u32[]{:S(2)}) async-start(bf16[16,8,2688]{2,1,0:T(8,128)(2,1)} %fusion.18), calls=%async_computation | async-start | bytes 1376256 | tf_op jit(solution)/shard_map/all_to_all | solution.py:81
  56.2 1.4 copy-start.2
  61.2 68.7 %copy-start.4 = (bf16[1,256,2560]{2,1,0:T(8,128)(2,1)S(1)}, bf16[1,256,2560]{2,1,0:T(8,128)(2,1)}, u32[]{:S(2)}) copy-start(bf16[1,256,2560]{2,1,0:T(8,128)(2,1)} %param.11) | copy-start | bytes 3932164
  127.6 2.3 copy-start.1
  129.9 2.5 copy-start.5
  143.0 8.2 %copy-start.3 = (f32[16,8,8]{0,2,1:T(8,128)S(1)}, f32[16,8,8]{0,2,1:T(8,128)}, u32[]{:S(2)}) copy-start(f32[16,8,8]{0,2,1:T(8,128)} %get-tuple-element.5) | copy-start | bytes 12292
  143.0 71.6 %all-to-all-start.2 = ((bf16[32,32,2560]{2,1,0:T(8,128)(2,1)}), bf16[32,32,2560]{2,1,0:T(8,128)(2,1)}, u32[]{:S(2)}, u32[]{:S(2)}) async-start(bf16[32,32,2560]{2,1,0:T(8,128)(2,1)} %bitcast.75), calls=%async_computation.2 | async-start | bytes 10485760 | tf_op jit(solution)/shard_map/all_to_all | solution.py:90

commit v2 on v0

v2 whole, which is shorter than its diff:
```python
import jax
import jax.numpy as jnp
from jax import lax
from jax.experimental import pallas as pl
from jax.experimental.pallas import tpu as pltpu
from jax.sharding import Mesh, PartitionSpec as P

TOP_GROUPS = 3
N_RG = 16
SHARDS = 4
LEXP = 8
CE = 2
CG = 8
COPIES = 2
META = 128
BF = jnp.bfloat16
F32 = jnp.float32
I32 = jnp.int32
HELD = N_RG * CG
SPREAD = LEXP * N_RG * CE
VMEM = pl.BlockSpec(memory_space=pltpu.VMEM)
ANY = pl.BlockSpec(memory_space=pl.ANY)


def iota(shape, dim):
    return lax.broadcasted_iota(I32, shape, dim)


def column(info, index):
    return info[:, index : index + 1]


def pack_kernel(groups, picks, gates, tokens, *refs):
    weights, (packed, slot), halves, (held, in_sems, out_sems) = refs[:3], refs[3:5], refs[5:7], refs[7:]
    tok, width = tokens.shape
    part = weights[0].shape[1] // 2
    inward, outward = [], []
    for i, weight in enumerate(weights):
        for j, half in enumerate(halves):
            here = held.at[j, pl.ds(i * part, part)]
            sem = in_sems.at[2 * i + j]
            inward.append(pltpu.make_async_copy(weight.at[0, pl.ds(j * part, part)], here, sem))
            there = half.at[pl.ds(i * part, part)]
            outward.append(pltpu.make_async_copy(here, there, out_sems.at[2 * i + j]))
    for copy in inward:
        copy.start()
    shape = (HELD, tok)
    group = iota(shape, 0) // CG
    row = iota(shape, 0) % CG
    heres = [(groups[k : k + 1, :] == group).astype(F32) for k in range(TOP_GROUPS)]
    member = heres[0] + heres[1] + heres[2]
    earlier = (iota((tok, tok), 0) < iota((tok, tok), 1)).astype(BF)
    rank = jnp.dot(member.astype(BF), earlier, preferred_element_type=F32)
    held = member * (rank == row.astype(F32)).astype(F32)
    slot[...] = held.astype(BF)

    def select(values, j):
        total = heres[0] * values[j : j + 1, :]
        for k in range(1, TOP_GROUPS):
            total = total + heres[k] * values[2 * k + j : 2 * k + j + 1, :]
        return jnp.sum(held * total, axis=1, keepdims=True)

    labels = picks[...].astype(F32) + 1.0
    probs = gates[...]
    for arrival, copy in zip(inward, outward):
        arrival.wait()
        copy.start()
    lane = iota((HELD, META), 1)
    cols = jnp.zeros((HELD, META), F32)
    for j in range(2):
        gate = select(probs, j)
        high = gate.astype(BF).astype(F32)
        low = (gate - high).astype(BF).astype(F32)
        least = gate - high - low
        for place, value in ((0, select(labels, j)), (2, high), (4, low), (6, least)):
            cols = jnp.where(lane == place + j, value, cols)
    packed[:, width:] = cols.astype(BF)
    packed[:, :width] = jnp.dot(held.astype(BF), tokens[...], preferred_element_type=F32).astype(BF)
    for copy in outward:
        copy.wait()


def pack(tokens, groups, picks, gates, w_gate, w_up, w_down):
    tok, width = tokens.shape
    part = w_gate.shape[1] // 2
    small = [groups.T, picks.T, gates.T, tokens]
    whole = lambda shape: pl.BlockSpec(shape, lambda i: (0,) * len(shape))
    struct = lambda *shape: jax.ShapeDtypeStruct(shape, BF)
    shapes = (struct(HELD, width + META), struct(HELD, tok))
    return pl.pallas_call(
        pack_kernel,
        grid=(1,),
        out_shape=shapes + (struct(3 * part, width),) * 2,
        in_specs=[whole(array.shape) for array in small] + [ANY] * 3,
        out_specs=tuple(whole(s.shape) for s in shapes) + (ANY,) * 2,
        scratch_shapes=[
            pltpu.VMEM((2, 3 * part, width), BF),
            pltpu.SemaphoreType.DMA((6,)),
            pltpu.SemaphoreType.DMA((6,)),
        ],
        compiler_params=pltpu.CompilerParams(vmem_limit_bytes=60 << 20),
        name="pack",
    )(*small, w_gate, w_up, w_down)


def places(cols):
    info = cols.astype(F32)
    shape = (HELD, SPREAD)
    slot = iota(shape, 1)
    label = (slot // (N_RG * CE) + 1).astype(F32)
    source = (slot // CE) % N_RG
    place = (slot % CE).astype(F32)
    same = (iota(shape, 0) // CG == source).astype(F32)
    one = same * (column(info, 0) == label).astype(F32)
    two = same * (column(info, 1) == label).astype(F32)
    hit = one + two
    earlier = (iota((HELD, HELD), 1) < iota((HELD, HELD), 0)).astype(BF)
    rank = jnp.dot(earlier, hit.astype(BF), preferred_element_type=F32)
    taken = (rank == place).astype(F32)
    gates = [column(info, 2 + j) + column(info, 4 + j) + column(info, 6 + j) for j in range(2)]
    return taken * hit, taken * (one * gates[0] + two * gates[1])


def spread_kernel(arrived, *refs):
    rows = refs[-1]
    width = rows.shape[1]
    chosen, _ = places(arrived[:, width:])
    sent = jnp.dot(
        chosen.T.astype(BF), arrived[:, :width], preferred_element_type=F32
    ).astype(BF)
    for copy in range(COPIES):
        rows[copy * SPREAD : (copy + 1) * SPREAD, :] = sent


def spread(arrived, *after):
    width = arrived.shape[1] - META
    return pl.pallas_call(
        spread_kernel,
        out_shape=jax.ShapeDtypeStruct((COPIES * SPREAD, width), BF),
        in_specs=[VMEM] + [ANY] * len(after),
        out_specs=VMEM,
        compiler_params=pltpu.CompilerParams(vmem_limit_bytes=16 << 20),
        cost_estimate=pl.CostEstimate(
            flops=2 * SPREAD * HELD * width, bytes_accessed=2 * 3 * HELD * width, transcendentals=0
        ),
        name="spread",
    )(arrived, *after)


def combine_kernel(cols, outs, mixed):
    _, scaled = places(cols[...])
    high = scaled.astype(BF)
    low = (scaled - high.astype(F32)).astype(BF)
    both = jnp.concatenate([high, low], axis=0)
    both = jnp.concatenate([both] * COPIES, axis=1)
    total = jnp.dot(both, outs[...], preferred_element_type=F32)
    mixed[...] = (total[:HELD] + total[HELD:]).astype(BF)


def combine(arrived, outs):
    rows, width = outs.shape
    whole = lambda rows: pl.BlockSpec((rows, width), lambda i: (0, 0))
    return pl.pallas_call(
        combine_kernel,
        grid=(1,),
        out_shape=jax.ShapeDtypeStruct((HELD, width), BF),
        in_specs=[pl.BlockSpec((HELD, META), lambda i: (0, width // META)), whole(rows)],
        out_specs=whole(HELD),
        compiler_params=pltpu.CompilerParams(vmem_limit_bytes=24 << 20),
        cost_estimate=pl.CostEstimate(
            flops=4 * rows * HELD * width, bytes_accessed=2 * 5 * HELD * width, transcendentals=0
        ),
        name="combine",
    )(arrived, outs)


def glu(gate_part, up_part):
    return (gate_part / (1.0 + jnp.exp(-gate_part)) * up_part).astype(BF)


def expert_kernel(rows, w_gate, w_up, w_down, first, second, outs, gate, up, down, sems):
    own = w_gate.shape[1]
    part = own // 2
    copies = []
    for i, (weight, here) in enumerate(((w_gate, gate), (w_up, up), (w_down, down))):
        block = pl.ds(i * part, part)
        sources = (weight.at[0], first.at[block], second.at[block])
        places = (pl.ds(0, own), pl.ds(own, part), pl.ds(own + part, part))
        copies.append(
            [
                pltpu.make_async_copy(source, here.at[place], sems.at[3 * i + j])
                for j, (source, place) in enumerate(zip(sources, places))
            ]
        )
    for group in copies:
        for copy in group:
            copy.start()
    contract = (((1,), (1,)), ((), ()))
    for copy in copies[0]:
        copy.wait()
    gate_part = lax.dot_general(rows[...], gate[...], contract, preferred_element_type=F32)
    for copy in copies[1]:
        copy.wait()
    up_part = lax.dot_general(rows[...], up[...], contract, preferred_element_type=F32)
    hidden = glu(gate_part, up_part)
    for copy in copies[2]:
        copy.wait()
    outs[...] = jnp.dot(hidden, down[...], preferred_element_type=F32).astype(BF)


def experts(rows, w_gate, w_up, w_down, first, second):
    width = rows.shape[1]
    hidden = 2 * w_gate.shape[1]
    return pl.pallas_call(
        expert_kernel,
        out_shape=jax.ShapeDtypeStruct(rows.shape, BF),
        in_specs=[VMEM] + [ANY] * 5,
        out_specs=VMEM,
        scratch_shapes=[pltpu.VMEM((hidden, width), BF)] * 3 + [pltpu.SemaphoreType.DMA((9,))],
        compiler_params=pltpu.CompilerParams(vmem_limit_bytes=40 << 20),
        cost_estimate=pl.CostEstimate(
            flops=6 * rows.shape[0] * hidden * width,
            bytes_accessed=6 * hidden * width + 4 * rows.shape[0] * width,
            transcendentals=rows.shape[0] * hidden,
        ),
        name="experts",
    )(rows, w_gate, w_up, w_down, first, second)


def unpack_kernel(slot, home, result):
    contract = (((0,), (0,)), ((), ()))
    result[...] = lax.dot_general(
        slot[...], home[...], contract, preferred_element_type=F32
    ).astype(BF)


def unpack(slot, home):
    return pl.pallas_call(
        unpack_kernel,
        out_shape=jax.ShapeDtypeStruct((slot.shape[1], home.shape[1]), BF),
        in_specs=[VMEM] * 2,
        out_specs=VMEM,
        compiler_params=pltpu.CompilerParams(vmem_limit_bytes=16 << 20),
        name="unpack",
    )(slot, home)


def ring(block, step):
    return lax.ppermute(block, ("h", "v"), [(i, (i + step) % SHARDS) for i in range(SHARDS)])


def along_z(rows):
    shape = rows.shape
    rows = rows.reshape(N_RG, CG, -1)
    return lax.all_to_all(rows, "z", 0, 0, tiled=True).reshape(shape)


def in_plane(rows):
    shape = rows.shape
    rows = rows.reshape(COPIES * LEXP, N_RG * CE, -1)
    return lax.all_to_all(rows, ("h", "x", "c"), 0, 0, tiled=True).reshape(shape)


def on_device(tokens, chosen_groups, local_picks, gate_probs, w_gate, w_up, w_down):
    packed, slot, first, second = pack(
        tokens, chosen_groups, local_picks, gate_probs, w_gate, w_up, w_down
    )
    first = ring(first, -1)
    second = ring(second, 1)
    arrived = lax.cond(lax.axis_index("z") < N_RG, along_z, lambda block: block, packed)
    rows = in_plane(spread(arrived, first, second))
    outs = experts(rows, w_gate, w_up, w_down, first, second)
    mixed = combine(arrived, in_plane(outs))
    return unpack(slot, along_z(mixed))


def solution(mesh):
    grid = Mesh(mesh.devices.reshape(N_RG, 2, 2, 4, 2), ("z", "h", "v", "x", "c"))
    every = ("z", "h", "v", "x", "c")
    weights = P(("x", "c"), ("z", "h", "v"), None)
    return jax.shard_map(
        on_device,
        mesh=grid,
        in_specs=(P(every, None),) * 4 + (weights,) * 3,
        out_specs=P(every, None),
        check_vma=False,
    )
```

time: 635 us -> 195 us (0.31)
  the two profiles are of different devices: /device:TPU:1 before, /device:TPU:32 now
where the time goes in v2:
time: 195 us; the launch traced here: 194 us
  blocking collectives  174 us (89%)
  Pallas kernels  13.7 us (7%)
  starting transfers between devices  6.84 us (4%)
    all_to_all x2, blocking collectives, along_z(): return lax.all_to_all(rows, 'z', 0, 0, tiled=True).reshape(shape)  95.7 us
    all_to_all x2, blocking collectives, in_plane(): lax.all_to_all(rows, ('h', 'x', 'c'), 0, 0, tiled=True).reshape(shape)  77.9 us
    ppermute x2, starting transfers between devices, ring(): lax.ppermute(block, ('h', 'v'), [(i, (i + step) % SHARDS) for i in range(...  6.84 us
    pallas_call x1, Pallas kernels, experts(): pl.pallas_call(expert_kernel, out_shape=jax.ShapeDtypeStruct(rows.shape,...  6.16 us
    pallas_call x1, Pallas kernels, pack(): pl.pallas_call(pack_kernel, grid=(1,), out_shape=shapes + (struct(3 * par...  4.79 us
  transfers between devices with their start and end apart: 2, of which 0 were waited for; matrix products, arithmetic and copies ran while one was open for 0% of the time, Pallas kernels for 0%

profile of v2, /device:TPU:32, one launch (start us, length us, event | category | flops | bytes accessed | tf_op | source)
XLA Modules:
  0.0 194.3 jit_solution(1152144551659263615)
XLA Ops:
  0.0 4.8 %pack.1 = (bf16[128,2688]{1,0:T(8,128)(2,1)S(1)}, bf16[128,32]{1,0:T(8,128)(2,1)}, bf16[384,2560]{1,0:T(8,128)(2,1)}, bf16[384,2560]{1,0:T(8,128)(2,1)}) custom-call(s32[3,32]{1,0:T(4,128)} %bitcast.21, s32[6,32]{1,0:T(8,128)} %bitcast.19, f32[6,32]{1,0:T(8,128)} %bitcast.20, bf16[32,2560]{1,0:T(8,128)(2,1)} %tokens.1, bf16[1,256,2560]{2,1,0:T(8,128)(2,1)} %w_gate.1, ...), custom_call_target="tpu_custom_call" | custom-call | tf_op jit(solution)/shard_map/pack/pallas_call | solution.py:90
  4.8 4.9 %collective-permute-start = (bf16[384,2560]{1,0:T(8,128)(2,1)}, bf16[384,2560]{1,0:T(8,128)(2,1)S(1)}, u32[]{:S(2)}, u32[]{:S(2)}) collective-permute-start(bf16[384,2560]{1,0:T(8,128)(2,1)} %get-tuple-element.16), channel_id=1, source_target_pairs={{0,24},{8,0},{16,8},{24,16},{1,25},{9,1},{17,9},{25,17},{2,26},{10... | collective-permute-start | bytes 5898248 | tf_op jit(solution)/shard_map/ppermute | solution.py:249
  9.7 1.9 collective-permute-start.1
  11.7 52.5 %conditional.1 = (bf16[128,2688]{1,0:T(8,128)(2,1)S(1)}) conditional(s32[]{:T(128)} %convert_element_type.3, bf16[128,2688]{1,0:T(8,128)(2,1)S(1)} %get-tuple-element.15, bf16[128,2688]{1,0:T(8,128)(2,1)S(1)} %get-tuple-element.15), branch_computations={%region_0.0_spmd, %region_1.0_spmd} | conditional | bytes 2752520 | solution.py:270
  11.7 52.5 %all_to_all.19 = bf16[16,8,2688]{2,1,0:T(8,128)(2,1)S(1)} all-to-all(bf16[16,8,2688]{2,1,0:T(8,128)(2,1)S(1)} %copy.10), channel_id=1, replica_groups=mesh['z'=16,'h'=2,'v'=2,'x'=4,'c'=2] {'z'}, dimensions={0} | all-to-all | bytes 1376256 | tf_op jit(solution)/shard_map/cond/branch_1_fun/all_to_all | solution.py:255
  64.2 0.0 collective-permute-done.refs_0_.first
  64.2 0.0 collective-permute-done.1.refs_1_.second
  64.2 0.8 spread.1
  65.0 0.0 copy-start
  65.0 0.0 copy-start.1
  65.0 0.0 copy-start.2
  65.0 40.4 %all_to_all.20 = bf16[16,32,2560]{2,1,0:T(8,128)(2,1)S(1)} all-to-all(bf16[16,32,2560]{2,1,0:T(8,128)(2,1)S(1)} %bitcast.11), channel_id=1, replica_groups=mesh['z'=16,'h'=2,'v'=2,'x'=4,'c'=2] {'h','x','c'}, dimensions={0} | all-to-all | bytes 5242880 | tf_op jit(solution)/shard_map/all_to_all | solution.py:261
  105.4 0.0 copy-done
  105.5 0.0 copy-done.1
  105.5 0.0 copy-done.2
  105.5 6.2 %experts.1 = bf16[512,2560]{1,0:T(8,128)(2,1)S(1)} custom-call(bf16[512,2560]{1,0:T(8,128)(2,1)S(1)} %bitcast.13, bf16[1,256,2560]{2,1,0:T(8,128)(2,1)S(1)} %copy-done, bf16[1,256,2560]{2,1,0:T(8,128)(2,1)S(1)} %copy-done.1, bf16[1,256,2560]{2,1,0:T(8,128)(2,1)S(1)} %copy-done.2, bf16[384,2560]{1,0:T(8,128)(2,1)S(1)} %collective-permute-done.refs_0_.first, ...), custom_call_target="tpu_custom_call" | custom-call | flops 4026531840 | bytes 13107200 | tf_op jit(solution)/shard_map/experts/pallas_call | solution.py:214
  111.6 37.5 %all_to_all.21 = bf16[16,32,2560]{2,1,0:T(8,128)(2,1)S(1)} all-to-all(bf16[16,32,2560]{2,1,0:T(8,128)(2,1)S(1)} %bitcast.14), channel_id=1, replica_groups=mesh['z'=16,'h'=2,'v'=2,'x'=4,'c'=2] {'h','x','c'}, dimensions={0} | all-to-all | bytes 5242880 | tf_op jit(solution)/shard_map/all_to_all | solution.py:261
  149.1 0.0 copy-start.3
  149.1 1.1 combine.1
  150.2 43.2 %all_to_all.22 = bf16[16,8,2560]{2,1,0:T(8,128)(2,1)S(1)} all-to-all(bf16[16,8,2560]{2,1,0:T(8,128)(2,1)S(1)} %bitcast.16), channel_id=1, replica_groups=mesh['z'=16,'h'=2,'v'=2,'x'=4,'c'=2] {'z'}, dimensions={0} | all-to-all | bytes 1310720 | tf_op jit(solution)/shard_map/all_to_all | solution.py:255
  193.4 0.0 copy-done.3
  193.4 0.9 unpack.1
  (1 shorter events, 0.0 us)
Async XLA Ops:
  4.8 59.4 %collective-permute-start = (bf16[384,2560]{1,0:T(8,128)(2,1)}, bf16[384,2560]{1,0:T(8,128)(2,1)S(1)}, u32[]{:S(2)}, u32[]{:S(2)}) collective-permute-start(bf16[384,2560]{1,0:T(8,128)(2,1)} %get-tuple-element.16), channel_id=1, source_target_pairs={{0,24},{8,0},{16,8},{24,16},{1,25},{9,1},{17,9},{25,17},{2,26},{10... | collective-permute-start | bytes 5898248 | tf_op jit(solution)/shard_map/ppermute | solution.py:249
  9.7 54.5 %collective-permute-start.1 = (bf16[384,2560]{1,0:T(8,128)(2,1)}, bf16[384,2560]{1,0:T(8,128)(2,1)}, u32[]{:S(2)}, u32[]{:S(2)}) collective-permute-start(bf16[384,2560]{1,0:T(8,128)(2,1)} %get-tuple-element.17), channel_id=1, source_target_pairs={{0,8},{8,16},{16,24},{24,0},{1,9},{9,17},{17,25},{25,1},{2,10},{10... | collective-permute-start | bytes 5898248 | tf_op jit(solution)/shard_map/ppermute | solution.py:249
  65.0 40.5 %copy-start = (bf16[1,256,2560]{2,1,0:T(8,128)(2,1)S(1)}, bf16[1,256,2560]{2,1,0:T(8,128)(2,1)}, u32[]{:S(2)}) copy-start(bf16[1,256,2560]{2,1,0:T(8,128)(2,1)} %w_gate.1) | copy-start | bytes 3932164
  65.0 40.5 %copy-start.1 = (bf16[1,256,2560]{2,1,0:T(8,128)(2,1)S(1)}, bf16[1,256,2560]{2,1,0:T(8,128)(2,1)}, u32[]{:S(2)}) copy-start(bf16[1,256,2560]{2,1,0:T(8,128)(2,1)} %w_up.1) | copy-start | bytes 3932164
  65.0 40.5 %copy-start.2 = (bf16[1,256,2560]{2,1,0:T(8,128)(2,1)S(1)}, bf16[1,256,2560]{2,1,0:T(8,128)(2,1)}, u32[]{:S(2)}) copy-start(bf16[1,256,2560]{2,1,0:T(8,128)(2,1)} %w_down.1) | copy-start | bytes 3932164
  149.1 44.3 %copy-start.3 = (bf16[128,32]{1,0:T(8,128)(2,1)S(1)}, bf16[128,32]{1,0:T(8,128)(2,1)}, u32[]{:S(2)}) copy-start(bf16[128,32]{1,0:T(8,128)(2,1)} %get-tuple-element.14.slot) | copy-start | bytes 24580

commit v3 on v2

--- a/solution.py
+++ b/solution.py
@@ -30,20 +30,7 @@
     return info[:, index : index + 1]
 
 
-def pack_kernel(groups, picks, gates, tokens, *refs):
-    weights, (packed, slot), halves, (held, in_sems, out_sems) = refs[:3], refs[3:5], refs[5:7], refs[7:]
-    tok, width = tokens.shape
-    part = weights[0].shape[1] // 2
-    inward, outward = [], []
-    for i, weight in enumerate(weights):
-        for j, half in enumerate(halves):
-            here = held.at[j, pl.ds(i * part, part)]
-            sem = in_sems.at[2 * i + j]
-            inward.append(pltpu.make_async_copy(weight.at[0, pl.ds(j * part, part)], here, sem))
-            there = half.at[pl.ds(i * part, part)]
-            outward.append(pltpu.make_async_copy(here, there, out_sems.at[2 * i + j]))
-    for copy in inward:
-        copy.start()
+def find_slots(groups, tok):
     shape = (HELD, tok)
     group = iota(shape, 0) // CG
     row = iota(shape, 0) % CG
@@ -52,7 +39,50 @@
     earlier = (iota((tok, tok), 0) < iota((tok, tok), 1)).astype(BF)
     rank = jnp.dot(member.astype(BF), earlier, preferred_element_type=F32)
     held = member * (rank == row.astype(F32)).astype(F32)
-    slot[...] = held.astype(BF)
+    return heres, held
+
+
+def halve_kernel(w_gate, w_up, w_down, first, second, held, in_sems, out_sems):
+    part = w_gate.shape[1] // 2
+    inward, outward = [], []
+    for i, weight in enumerate((w_gate, w_up, w_down)):
+        for j, half in enumerate((first, second)):
+            here = held.at[j, pl.ds(i * part, part)]
+            sem = in_sems.at[2 * i + j]
+            inward.append(pltpu.make_async_copy(weight.at[0, pl.ds(j * part, part)], here, sem))
+            there = half.at[pl.ds(i * part, part)]
+            outward.append(pltpu.make_async_copy(here, there, out_sems.at[2 * i + j]))
+    for copy in inward:
+        copy.start()
+    for arrival, copy in zip(inward, outward):
+        arrival.wait()
+        copy.start()
+    for copy in outward:
+        copy.wait()
+
+
+def halve(w_gate, w_up, w_down):
+    _, hidden, width = w_gate.shape
+    half = jax.ShapeDtypeStruct((3 * hidden // 2, width), BF)
+    return pl.pallas_call(
+        halve_kernel,
+        out_shape=(half, half),
+        in_specs=[ANY] * 3,
+        out_specs=(ANY, ANY),
+        scratch_shapes=[
+            pltpu.VMEM((2,) + half.shape, BF),
+            pltpu.SemaphoreType.DMA((6,)),
+            pltpu.SemaphoreType.DMA((6,)),
+        ],
+        compiler_params=pltpu.CompilerParams(vmem_limit_bytes=60 << 20),
+        name="halve",
+    )(w_gate, w_up, w_down)
+
+
+def pack_kernel(groups, picks, gates, tokens, *refs):
+    packed = refs[-1]
+    tok, width = tokens.shape
+    heres, held = find_slots(groups, tok)
 
     def select(values, j):
         total = heres[0] * values[j : j + 1, :]
@@ -62,9 +92,6 @@
 
     labels = picks[...].astype(F32) + 1.0
     probs = gates[...]
-    for arrival, copy in zip(inward, outward):
-        arrival.wait()
-        copy.start()
     lane = iota((HELD, META), 1)
     cols = jnp.zeros((HELD, META), F32)
     for j in range(2):
@@ -76,31 +103,38 @@
             cols = jnp.where(lane == place + j, value, cols)
     packed[:, width:] = cols.astype(BF)
     packed[:, :width] = jnp.dot(held.astype(BF), tokens[...], preferred_element_type=F32).astype(BF)
-    for copy in outward:
-        copy.wait()
-
-
-def pack(tokens, groups, picks, gates, w_gate, w_up, w_down):
+
+
+def pack(tokens, groups, picks, gates, *after):
     tok, width = tokens.shape
-    part = w_gate.shape[1] // 2
     small = [groups.T, picks.T, gates.T, tokens]
     whole = lambda shape: pl.BlockSpec(shape, lambda i: (0,) * len(shape))
-    struct = lambda *shape: jax.ShapeDtypeStruct(shape, BF)
-    shapes = (struct(HELD, width + META), struct(HELD, tok))
+    out = jax.ShapeDtypeStruct((HELD, width + META), BF)
     return pl.pallas_call(
         pack_kernel,
         grid=(1,),
-        out_shape=shapes + (struct(3 * part, width),) * 2,
-        in_specs=[whole(array.shape) for array in small] + [ANY] * 3,
-        out_specs=tuple(whole(s.shape) for s in shapes) + (ANY,) * 2,
-        scratch_shapes=[
-            pltpu.VMEM((2, 3 * part, width), BF),
-            pltpu.SemaphoreType.DMA((6,)),
-            pltpu.SemaphoreType.DMA((6,)),
-        ],
-        compiler_params=pltpu.CompilerParams(vmem_limit_bytes=60 << 20),
+        out_shape=out,
+        in_specs=[whole(array.shape) for array in small] + [ANY] * len(after),
+        out_specs=whole(out.shape),
+        compiler_params=pltpu.CompilerParams(vmem_limit_bytes=56 << 20),
         name="pack",
-    )(*small, w_gate, w_up, w_down)
+    )(*small, *after)
+
+
+def slots_kernel(groups, *refs):
+    slot = refs[-1]
+    slot[...] = find_slots(groups, slot.shape[1])[1].astype(BF)
+
+
+def slots(groups, *after):
+    return pl.pallas_call(
+        slots_kernel,
+        out_shape=jax.ShapeDtypeStruct((HELD, groups.shape[0]), BF),
+        in_specs=[VMEM] + [ANY] * len(after),
+        out_specs=VMEM,
+        compiler_params=pltpu.CompilerParams(vmem_limit_bytes=8 << 20),
+        name="slots",
+    )(groups.T, *after)
 
 
 def places(cols):
@@ -262,16 +296,15 @@
 
 
 def on_device(tokens, chosen_groups, local_picks, gate_probs, w_gate, w_up, w_down):
-    packed, slot, first, second = pack(
-        tokens, chosen_groups, local_picks, gate_probs, w_gate, w_up, w_down
-    )
+    first, second = halve(w_gate, w_up, w_down)
+    packed = pack(tokens, chosen_groups, local_picks, gate_probs, first, second)
     first = ring(first, -1)
     second = ring(second, 1)
     arrived = lax.cond(lax.axis_index("z") < N_RG, along_z, lambda block: block, packed)
     rows = in_plane(spread(arrived, first, second))
     outs = experts(rows, w_gate, w_up, w_down, first, second)
     mixed = combine(arrived, in_plane(outs))
-    return unpack(slot, along_z(mixed))
+    return unpack(slots(chosen_groups, mixed), along_z(mixed))
 
 
 def solution(mesh):

time: 195 us -> 191 us (0.979)
  blocking collectives: 174 us -> 130 us
  waiting for transfers between devices: 0.01 us -> 33.2 us
  starting transfers between devices: 6.84 us -> 12.8 us
    all_to_all x2 -> x1, blocking collectives: 95.7 us -> 52.4 us  [along_z(): return lax.all_to_all(rows, 'z', 0, 0, tiled=True).reshape(shape)]
    all_to_all x0 -> x1, waiting for transfers between devices: none -> 33.2 us  [along_z(): return lax.all_to_all(rows, 'z', 0, 0, tiled=True).reshape(shape)]
    all_to_all x0 -> x1, starting transfers between devices: none -> 5.93 us  [along_z(): return lax.all_to_all(rows, 'z', 0, 0, tiled=True).reshape(shape)]
    pallas_call x1 -> x3, Pallas kernels: 4.79 us -> 4.77 us  [the longest x1 3.21 us: halve(): pl.pallas_call(halve_kernel, out_shape=(half, half), in_specs=[ANY] * 3,...]
  transfers between devices with their start and end apart: 2 -> 3, of which waited for: 0 -> 1; matrix products, arithmetic and copies ran while one was open for 0% -> 0% of each run, Pallas kernels for 0% -> 1%
where the time goes in v3:
time: 191 us
  blocking collectives  130 us (68%)
  waiting for transfers between devices  33.2 us (17%)
  Pallas kernels  14.5 us (8%)
  starting transfers between devices  12.8 us (7%)
    all_to_all x2, blocking collectives, in_plane(): lax.all_to_all(rows, ('h', 'x', 'c'), 0, 0, tiled=True).reshape(shape)  77.9 us
    all_to_all x1, blocking collectives, along_z(): return lax.all_to_all(rows, 'z', 0, 0, tiled=True).reshape(shape)  52.4 us
    all_to_all x1, waiting for transfers between devices, along_z(): return lax.all_to_all(rows, 'z', 0, 0, tiled=True).reshape(shape)  33.2 us
    ppermute x2, starting transfers between devices, ring(): lax.ppermute(block, ('h', 'v'), [(i, (i + step) % SHARDS) for i in range(...  6.84 us
    pallas_call x1, Pallas kernels, experts(): pl.pallas_call(expert_kernel, out_shape=jax.ShapeDtypeStruct(rows.shape,...  6.16 us
    all_to_all x1, starting transfers between devices, along_z(): return lax.all_to_all(rows, 'z', 0, 0, tiled=True).reshape(shape)  5.93 us
  transfers between devices with their start and end apart: 3, of which 1 were waited for; matrix products, arithmetic and copies ran while one was open for 0% of the time, Pallas kernels for 1%

profile of v3, /device:TPU:32, one launch (start us, length us, event | category | flops | bytes accessed | tf_op | source)
XLA Modules:
  0.0 191.1 jit_solution(3086304066507791546)
XLA Ops:
  0.0 3.2 %halve.1 = (bf16[384,2560]{1,0:T(8,128)(2,1)}, bf16[384,2560]{1,0:T(8,128)(2,1)}) custom-call(bf16[1,256,2560]{2,1,0:T(8,128)(2,1)} %w_gate.3, bf16[1,256,2560]{2,1,0:T(8,128)(2,1)} %w_up.3, bf16[1,256,2560]{2,1,0:T(8,128)(2,1)} %w_down.3), custom_call_target="tpu_custom_call" | custom-call | tf_op jit(solution)/shard_map/halve/pallas_call | solution.py:67
  3.2 4.9 %collective-permute-start = (bf16[384,2560]{1,0:T(8,128)(2,1)}, bf16[384,2560]{1,0:T(8,128)(2,1)S(1)}, u32[]{:S(2)}, u32[]{:S(2)}) collective-permute-start(bf16[384,2560]{1,0:T(8,128)(2,1)} %get-tuple-element.12.refs_0_), channel_id=1, source_target_pairs={{0,24},{8,0},{16,8},{24,16},{1,25},{9,1},{17,9},{25,17},{2,26},{10... | collective-permute-start | bytes 5898248 | tf_op jit(solution)/shard_map/ppermute | solution.py:283
  8.2 1.9 %collective-permute-start.1 = (bf16[384,2560]{1,0:T(8,128)(2,1)}, bf16[384,2560]{1,0:T(8,128)(2,1)}, u32[]{:S(2)}, u32[]{:S(2)}) collective-permute-start(bf16[384,2560]{1,0:T(8,128)(2,1)} %get-tuple-element.13.refs_1_), channel_id=1, source_target_pairs={{0,8},{8,16},{16,24},{24,0},{1,9},{9,17},{17,25},{25,1},{2,10},{10... | collective-permute-start | bytes 5898248 | tf_op jit(solution)/shard_map/ppermute | solution.py:283
  10.1 1.4 pack.1
  11.5 52.5 %conditional.1 = (bf16[128,2688]{1,0:T(8,128)(2,1)S(1)}) conditional(s32[]{:T(128)} %convert_element_type.3, bf16[128,2688]{1,0:T(8,128)(2,1)S(1)} %pack.1, bf16[128,2688]{1,0:T(8,128)(2,1)S(1)} %pack.1), branch_computations={%region_0.0_spmd, %region_1.0_spmd} | conditional | bytes 2752520 | solution.py:303
  11.6 52.4 %all_to_all.19 = bf16[16,8,2688]{2,1,0:T(8,128)(2,1)S(1)} all-to-all(bf16[16,8,2688]{2,1,0:T(8,128)(2,1)S(1)} %copy.10), channel_id=1, replica_groups=mesh['z'=16,'h'=2,'v'=2,'x'=4,'c'=2] {'z'}, dimensions={0} | all-to-all | bytes 1376256 | tf_op jit(solution)/shard_map/cond/branch_1_fun/all_to_all | solution.py:289
  64.0 0.0 collective-permute-done.refs_0_.first
  64.0 0.0 collective-permute-done.1.refs_1_.second
  64.0 0.8 spread.1
  64.8 0.0 copy-start
  64.8 0.0 copy-start.1
  64.8 0.0 copy-start.2
  64.8 40.4 %all_to_all.20 = bf16[16,32,2560]{2,1,0:T(8,128)(2,1)S(1)} all-to-all(bf16[16,32,2560]{2,1,0:T(8,128)(2,1)S(1)} %bitcast.11), channel_id=1, replica_groups=mesh['z'=16,'h'=2,'v'=2,'x'=4,'c'=2] {'h','x','c'}, dimensions={0} | all-to-all | bytes 5242880 | tf_op jit(solution)/shard_map/all_to_all | solution.py:295
  105.3 0.0 copy-done
  105.3 0.0 copy-done.1
  105.3 0.0 copy-done.2
  105.3 6.2 %experts.1 = bf16[512,2560]{1,0:T(8,128)(2,1)S(1)} custom-call(bf16[512,2560]{1,0:T(8,128)(2,1)S(1)} %bitcast.13, bf16[1,256,2560]{2,1,0:T(8,128)(2,1)S(1)} %copy-done, bf16[1,256,2560]{2,1,0:T(8,128)(2,1)S(1)} %copy-done.1, bf16[1,256,2560]{2,1,0:T(8,128)(2,1)S(1)} %copy-done.2, bf16[384,2560]{1,0:T(8,128)(2,1)S(1)} %collective-permute-done.refs_0_.first, ...), custom_call_target="tpu_custom_call" | custom-call | flops 4026531840 | bytes 13107200 | tf_op jit(solution)/shard_map/experts/pallas_call | solution.py:248
  111.4 37.5 %all_to_all.21 = bf16[16,32,2560]{2,1,0:T(8,128)(2,1)S(1)} all-to-all(bf16[16,32,2560]{2,1,0:T(8,128)(2,1)S(1)} %bitcast.14), channel_id=1, replica_groups=mesh['z'=16,'h'=2,'v'=2,'x'=4,'c'=2] {'h','x','c'}, dimensions={0} | all-to-all | bytes 5242880 | tf_op jit(solution)/shard_map/all_to_all | solution.py:295
  148.9 0.0 copy-start.3
  148.9 1.9 combine.1.refs_0_
  150.8 5.9 %all-to-all-start.3 = ((bf16[16,8,2560]{2,1,0:T(8,128)(2,1)}), bf16[16,8,2560]{2,1,0:T(8,128)(2,1)S(1)}, u32[]{:S(2)}, u32[]{:S(2)}) async-start(bf16[16,8,2560]{2,1,0:T(8,128)(2,1)} %bitcast.9), calls=%async_computation.3 | async-start | bytes 1310720 | tf_op jit(solution)/shard_map/all_to_all | solution.py:289
  156.8 0.0 copy-done.3
  156.8 0.1 slots.1.slot
  156.9 33.2 %all-to-all-done.3 = bf16[16,8,2560]{2,1,0:T(8,128)(2,1)S(1)} async-done(((bf16[16,8,2560]{2,1,0:T(8,128)(2,1)}), bf16[16,8,2560]{2,1,0:T(8,128)(2,1)S(1)}, u32[]{:S(2)}, u32[]{:S(2)}) %all-to-all-start.3) | async-done | bytes 655392 | tf_op jit(solution)/shard_map/all_to_all | solution.py:289
  190.2 0.9 unpack.1
  (1 shorter events, 0.0 us)
Async XLA Ops:
  3.2 60.8 %collective-permute-start = (bf16[384,2560]{1,0:T(8,128)(2,1)}, bf16[384,2560]{1,0:T(8,128)(2,1)S(1)}, u32[]{:S(2)}, u32[]{:S(2)}) collective-permute-start(bf16[384,2560]{1,0:T(8,128)(2,1)} %get-tuple-element.12.refs_0_), channel_id=1, source_target_pairs={{0,24},{8,0},{16,8},{24,16},{1,25},{9,1},{17,9},{25,17},{2,26},{10... | collective-permute-start | bytes 5898248 | tf_op jit(solution)/shard_map/ppermute | solution.py:283
  8.2 55.9 %collective-permute-start.1 = (bf16[384,2560]{1,0:T(8,128)(2,1)}, bf16[384,2560]{1,0:T(8,128)(2,1)}, u32[]{:S(2)}, u32[]{:S(2)}) collective-permute-start(bf16[384,2560]{1,0:T(8,128)(2,1)} %get-tuple-element.13.refs_1_), channel_id=1, source_target_pairs={{0,8},{8,16},{16,24},{24,0},{1,9},{9,17},{17,25},{25,1},{2,10},{10... | collective-permute-start | bytes 5898248 | tf_op jit(solution)/shard_map/ppermute | solution.py:283
  64.8 40.5 %copy-start = (bf16[1,256,2560]{2,1,0:T(8,128)(2,1)S(1)}, bf16[1,256,2560]{2,1,0:T(8,128)(2,1)}, u32[]{:S(2)}) copy-start(bf16[1,256,2560]{2,1,0:T(8,128)(2,1)} %w_gate.3) | copy-start | bytes 3932164
  64.8 40.5 %copy-start.1 = (bf16[1,256,2560]{2,1,0:T(8,128)(2,1)S(1)}, bf16[1,256,2560]{2,1,0:T(8,128)(2,1)}, u32[]{:S(2)}) copy-start(bf16[1,256,2560]{2,1,0:T(8,128)(2,1)} %w_up.3) | copy-start | bytes 3932164
  64.8 40.4 %copy-start.2 = (bf16[1,256,2560]{2,1,0:T(8,128)(2,1)S(1)}, bf16[1,256,2560]{2,1,0:T(8,128)(2,1)}, u32[]{:S(2)}) copy-start(bf16[1,256,2560]{2,1,0:T(8,128)(2,1)} %w_down.3) | copy-start | bytes 3932164
  148.9 7.8 %copy-start.3 = (s32[32,3]{0,1:T(4,128)S(1)}, s32[32,3]{0,1:T(4,128)}, u32[]{:S(2)}) copy-start(s32[32,3]{0,1:T(4,128)} %param.10) | copy-start | bytes 1156
  150.8 39.3 %all-to-all-start.3 = ((bf16[16,8,2560]{2,1,0:T(8,128)(2,1)}), bf16[16,8,2560]{2,1,0:T(8,128)(2,1)S(1)}, u32[]{:S(2)}, u32[]{:S(2)}) async-start(bf16[16,8,2560]{2,1,0:T(8,128)(2,1)} %bitcast.9), calls=%async_computation.3 | async-start | bytes 1310720 | tf_op jit(solution)/shard_map/all_to_all | solution.py:289

commit v4 on v3

--- a/solution.py
+++ b/solution.py
@@ -42,16 +42,18 @@
     return heres, held
 
 
-def halve_kernel(w_gate, w_up, w_down, first, second, held, in_sems, out_sems):
+def stack_kernel(w_gate, w_up, w_down, stacked, held, in_sems, out_sems):
     part = w_gate.shape[1] // 2
     inward, outward = [], []
     for i, weight in enumerate((w_gate, w_up, w_down)):
-        for j, half in enumerate((first, second)):
-            here = held.at[j, pl.ds(i * part, part)]
-            sem = in_sems.at[2 * i + j]
-            inward.append(pltpu.make_async_copy(weight.at[0, pl.ds(j * part, part)], here, sem))
-            there = half.at[pl.ds(i * part, part)]
-            outward.append(pltpu.make_async_copy(here, there, out_sems.at[2 * i + j]))
+        for j in range(2):
+            block = pl.ds((2 * i + j) * part, part)
+            source = weight.at[0, pl.ds(j * part, part)]
+            sem = 2 * i + j
+            inward.append(pltpu.make_async_copy(source, held.at[block], in_sems.at[sem]))
+            outward.append(
+                pltpu.make_async_copy(held.at[block], stacked.at[block], out_sems.at[sem])
+            )
     for copy in inward:
         copy.start()
     for arrival, copy in zip(inward, outward):
@@ -61,21 +63,21 @@
         copy.wait()
 
 
-def halve(w_gate, w_up, w_down):
+def stack(w_gate, w_up, w_down):
     _, hidden, width = w_gate.shape
-    half = jax.ShapeDtypeStruct((3 * hidden // 2, width), BF)
-    return pl.pallas_call(
-        halve_kernel,
-        out_shape=(half, half),
+    whole = (3 * hidden, width)
+    return pl.pallas_call(
+        stack_kernel,
+        out_shape=jax.ShapeDtypeStruct(whole, BF),
         in_specs=[ANY] * 3,
-        out_specs=(ANY, ANY),
+        out_specs=ANY,
         scratch_shapes=[
-            pltpu.VMEM((2,) + half.shape, BF),
+            pltpu.VMEM(whole, BF),
             pltpu.SemaphoreType.DMA((6,)),
             pltpu.SemaphoreType.DMA((6,)),
         ],
         compiler_params=pltpu.CompilerParams(vmem_limit_bytes=60 << 20),
-        name="halve",
+        name="stack",
     )(w_gate, w_up, w_down)
 
 
@@ -212,18 +214,15 @@
     return (gate_part / (1.0 + jnp.exp(-gate_part)) * up_part).astype(BF)
 
 
-def expert_kernel(rows, w_gate, w_up, w_down, first, second, outs, gate, up, down, sems):
+def expert_kernel(rows, w_gate, w_up, w_down, other, outs, gate, up, down, sems):
     own = w_gate.shape[1]
-    part = own // 2
     copies = []
     for i, (weight, here) in enumerate(((w_gate, gate), (w_up, up), (w_down, down))):
-        block = pl.ds(i * part, part)
-        sources = (weight.at[0], first.at[block], second.at[block])
-        places = (pl.ds(0, own), pl.ds(own, part), pl.ds(own + part, part))
+        sources = (weight.at[0], other.at[pl.ds(i * own, own)])
         copies.append(
             [
-                pltpu.make_async_copy(source, here.at[place], sems.at[3 * i + j])
-                for j, (source, place) in enumerate(zip(sources, places))
+                pltpu.make_async_copy(source, here.at[pl.ds(j * own, own)], sems.at[2 * i + j])
+                for j, source in enumerate(sources)
             ]
         )
     for group in copies:
@@ -242,15 +241,15 @@
     outs[...] = jnp.dot(hidden, down[...], preferred_element_type=F32).astype(BF)
 
 
-def experts(rows, w_gate, w_up, w_down, first, second):
+def experts(rows, w_gate, w_up, w_down, other):
     width = rows.shape[1]
     hidden = 2 * w_gate.shape[1]
     return pl.pallas_call(
         expert_kernel,
         out_shape=jax.ShapeDtypeStruct(rows.shape, BF),
-        in_specs=[VMEM] + [ANY] * 5,
+        in_specs=[VMEM] + [ANY] * 4,
         out_specs=VMEM,
-        scratch_shapes=[pltpu.VMEM((hidden, width), BF)] * 3 + [pltpu.SemaphoreType.DMA((9,))],
+        scratch_shapes=[pltpu.VMEM((hidden, width), BF)] * 3 + [pltpu.SemaphoreType.DMA((6,))],
         compiler_params=pltpu.CompilerParams(vmem_limit_bytes=40 << 20),
         cost_estimate=pl.CostEstimate(
             flops=6 * rows.shape[0] * hidden * width,
@@ -258,7 +257,7 @@
             transcendentals=rows.shape[0] * hidden,
         ),
         name="experts",
-    )(rows, w_gate, w_up, w_down, first, second)
+    )(rows, w_gate, w_up, w_down, other)
 
 
 def unpack_kernel(slot, home, result):
@@ -279,8 +278,13 @@
     )(slot, home)
 
 
-def ring(block, step):
-    return lax.ppermute(block, ("h", "v"), [(i, (i + step) % SHARDS) for i in range(SHARDS)])
+def from_neighbour(block):
+    pairs = [
+        (2 * y + core, 2 * ((y + step) % SHARDS) + core)
+        for y in range(SHARDS)
+        for core, step in ((0, -1), (1, 1))
+    ]
+    return lax.ppermute(block, ("h", "v", "c"), pairs)
 
 
 def along_z(rows):
@@ -296,13 +300,12 @@
 
 
 def on_device(tokens, chosen_groups, local_picks, gate_probs, w_gate, w_up, w_down):
-    first, second = halve(w_gate, w_up, w_down)
-    packed = pack(tokens, chosen_groups, local_picks, gate_probs, first, second)
-    first = ring(first, -1)
-    second = ring(second, 1)
+    stacked = stack(w_gate, w_up, w_down)
+    packed = pack(tokens, chosen_groups, local_picks, gate_probs, stacked)
+    other = from_neighbour(stacked)
     arrived = lax.cond(lax.axis_index("z") < N_RG, along_z, lambda block: block, packed)
-    rows = in_plane(spread(arrived, first, second))
-    outs = experts(rows, w_gate, w_up, w_down, first, second)
+    rows = in_plane(spread(arrived, other))
+    outs = experts(rows, w_gate, w_up, w_down, other)
     mixed = combine(arrived, in_plane(outs))
     return unpack(slots(chosen_groups, mixed), along_z(mixed))
 

time: 191 us -> 190 us (level)
  the two profiles are of different devices: /device:TPU:32 before, /device:TPU:40 now
where the time goes in v4:
time: 190 us; the launch traced here: 189 us
  blocking collectives  131 us (69%)
  waiting for transfers between devices  33.2 us (17%)
  Pallas kernels  14.5 us (8%)
  starting transfers between devices  10.8 us (6%)
    all_to_all x2, blocking collectives, in_plane(): lax.all_to_all(rows, ('h', 'x', 'c'), 0, 0, tiled=True).reshape(shape)  77.1 us
    all_to_all x1, blocking collectives, along_z(): return lax.all_to_all(rows, 'z', 0, 0, tiled=True).reshape(shape)  53.5 us
    all_to_all x1, waiting for transfers between devices, along_z(): return lax.all_to_all(rows, 'z', 0, 0, tiled=True).reshape(shape)  33.2 us
    all_to_all x1, starting transfers between devices, along_z(): return lax.all_to_all(rows, 'z', 0, 0, tiled=True).reshape(shape)  8.48 us
    pallas_call x1, Pallas kernels, experts(): pl.pallas_call(expert_kernel, out_shape=jax.ShapeDtypeStruct(rows.shape,...  6.15 us
  transfers between devices with their start and end apart: 2, of which 1 were waited for; matrix products, arithmetic and copies ran while one was open for 0% of the time, Pallas kernels for 1%

profile of v4, /device:TPU:40, one launch (start us, length us, event | category | flops | bytes accessed | tf_op | source)
XLA Modules:
  0.0 189.3 jit_solution(7569132052256692999)
XLA Ops:
  0.0 3.2 %stack.1.refs_0_ = bf16[768,2560]{1,0:T(8,128)(2,1)} custom-call(bf16[1,256,2560]{2,1,0:T(8,128)(2,1)} %w_gate.3, bf16[1,256,2560]{2,1,0:T(8,128)(2,1)} %w_up.3, bf16[1,256,2560]{2,1,0:T(8,128)(2,1)} %w_down.3), custom_call_target="tpu_custom_call" | custom-call | tf_op jit(solution)/shard_map/stack/pallas_call | solution.py:69
  3.2 2.4 %collective-permute-start = (bf16[768,2560]{1,0:T(8,128)(2,1)}, bf16[768,2560]{1,0:T(8,128)(2,1)}, u32[]{:S(2)}, u32[]{:S(2)}) collective-permute-start(bf16[768,2560]{1,0:T(8,128)(2,1)} %stack.1.refs_0_), channel_id=1, source_target_pairs={{0,24},{1,9},{8,0},{9,17},{16,8},{17,25},{24,16},{25,1},{2,26},{3,... | collective-permute-start | bytes 11796488 | tf_op jit(solution)/shard_map/ppermute | solution.py:287
  5.6 1.4 pack.1
  7.0 53.5 %conditional.1 = (bf16[128,2688]{1,0:T(8,128)(2,1)S(1)}) conditional(s32[]{:T(128)} %convert_element_type.3, bf16[128,2688]{1,0:T(8,128)(2,1)S(1)} %pack.1, bf16[128,2688]{1,0:T(8,128)(2,1)S(1)} %pack.1), branch_computations={%region_0.0_spmd, %region_1.0_spmd} | conditional | bytes 2752520 | solution.py:306
  7.1 53.5 %all_to_all.19 = bf16[16,8,2688]{2,1,0:T(8,128)(2,1)S(1)} all-to-all(bf16[16,8,2688]{2,1,0:T(8,128)(2,1)S(1)} %copy.10), channel_id=1, replica_groups=mesh['z'=16,'h'=2,'v'=2,'x'=4,'c'=2] {'z'}, dimensions={0} | all-to-all | bytes 1376256 | tf_op jit(solution)/shard_map/cond/branch_1_fun/all_to_all | solution.py:293
  60.5 0.0 collective-permute-done.refs_0_.other
  60.5 0.8 spread.1
  61.3 0.0 copy-start
  61.3 0.0 copy-start.1
  61.3 0.0 copy-start.2
  61.3 39.6 %all_to_all.20 = bf16[16,32,2560]{2,1,0:T(8,128)(2,1)S(1)} all-to-all(bf16[16,32,2560]{2,1,0:T(8,128)(2,1)S(1)} %bitcast.11), channel_id=1, replica_groups=mesh['z'=16,'h'=2,'v'=2,'x'=4,'c'=2] {'h','x','c'}, dimensions={0} | all-to-all | bytes 5242880 | tf_op jit(solution)/shard_map/all_to_all | solution.py:299
  100.9 0.0 copy-done
  100.9 0.0 copy-done.1
  100.9 0.0 copy-done.2
  100.9 6.2 %experts.1 = bf16[512,2560]{1,0:T(8,128)(2,1)S(1)} custom-call(bf16[512,2560]{1,0:T(8,128)(2,1)S(1)} %bitcast.13, bf16[1,256,2560]{2,1,0:T(8,128)(2,1)S(1)} %copy-done, bf16[1,256,2560]{2,1,0:T(8,128)(2,1)S(1)} %copy-done.1, bf16[1,256,2560]{2,1,0:T(8,128)(2,1)S(1)} %copy-done.2, bf16[768,2560]{1,0:T(8,128)(2,1)} %collective-permute-done.refs_0_.other), custom_call_target="tpu_custom_call" | custom-call | flops 4026531840 | bytes 13107200 | tf_op jit(solution)/shard_map/experts/pallas_call | solution.py:247
  107.1 37.5 %all_to_all.21 = bf16[16,32,2560]{2,1,0:T(8,128)(2,1)S(1)} all-to-all(bf16[16,32,2560]{2,1,0:T(8,128)(2,1)S(1)} %bitcast.14), channel_id=1, replica_groups=mesh['z'=16,'h'=2,'v'=2,'x'=4,'c'=2] {'h','x','c'}, dimensions={0} | all-to-all | bytes 5242880 | tf_op jit(solution)/shard_map/all_to_all | solution.py:299
  144.6 0.0 copy-start.3
  144.6 1.9 %combine.1.refs_0_ = bf16[128,2560]{1,0:T(8,128)(2,1)} custom-call(bf16[128,2688]{1,0:T(8,128)(2,1)S(1)} %get-tuple-element.10.arrived.cols, bf16[512,2560]{1,0:T(8,128)(2,1)S(1)} %bitcast.12), custom_call_target="tpu_custom_call" | custom-call | flops 671088640 | bytes 3276800 | tf_op jit(solution)/shard_map/combine/pallas_call | solution.py:199
  146.5 8.5 %all-to-all-start.3 = ((bf16[16,8,2560]{2,1,0:T(8,128)(2,1)}), bf16[16,8,2560]{2,1,0:T(8,128)(2,1)S(1)}, u32[]{:S(2)}, u32[]{:S(2)}) async-start(bf16[16,8,2560]{2,1,0:T(8,128)(2,1)} %bitcast.9), calls=%async_computation.3 | async-start | bytes 1310720 | tf_op jit(solution)/shard_map/all_to_all | solution.py:293
  155.0 0.0 copy-done.3
  155.0 0.1 slots.1.slot
  155.1 33.2 %all-to-all-done.3 = bf16[16,8,2560]{2,1,0:T(8,128)(2,1)S(1)} async-done(((bf16[16,8,2560]{2,1,0:T(8,128)(2,1)}), bf16[16,8,2560]{2,1,0:T(8,128)(2,1)S(1)}, u32[]{:S(2)}, u32[]{:S(2)}) %all-to-all-start.3) | async-done | bytes 655392 | tf_op jit(solution)/shard_map/all_to_all | solution.py:293
  188.3 0.9 unpack.1
  (1 shorter events, 0.0 us)
Async XLA Ops:
  3.2 57.3 %collective-permute-start = (bf16[768,2560]{1,0:T(8,128)(2,1)}, bf16[768,2560]{1,0:T(8,128)(2,1)}, u32[]{:S(2)}, u32[]{:S(2)}) collective-permute-start(bf16[768,2560]{1,0:T(8,128)(2,1)} %stack.1.refs_0_), channel_id=1, source_target_pairs={{0,24},{1,9},{8,0},{9,17},{16,8},{17,25},{24,16},{25,1},{2,26},{3,... | collective-permute-start | bytes 11796488 | tf_op jit(solution)/shard_map/ppermute | solution.py:287
  61.3 39.6 %copy-start = (bf16[1,256,2560]{2,1,0:T(8,128)(2,1)S(1)}, bf16[1,256,2560]{2,1,0:T(8,128)(2,1)}, u32[]{:S(2)}) copy-start(bf16[1,256,2560]{2,1,0:T(8,128)(2,1)} %w_gate.3) | copy-start | bytes 3932164
  61.3 39.6 %copy-start.1 = (bf16[1,256,2560]{2,1,0:T(8,128)(2,1)S(1)}, bf16[1,256,2560]{2,1,0:T(8,128)(2,1)}, u32[]{:S(2)}) copy-start(bf16[1,256,2560]{2,1,0:T(8,128)(2,1)} %w_up.3) | copy-start | bytes 3932164
  61.3 39.6 %copy-start.2 = (bf16[1,256,2560]{2,1,0:T(8,128)(2,1)S(1)}, bf16[1,256,2560]{2,1,0:T(8,128)(2,1)}, u32[]{:S(2)}) copy-start(bf16[1,256,2560]{2,1,0:T(8,128)(2,1)} %w_down.3) | copy-start | bytes 3932164
  144.6 10.4 %copy-start.3 = (s32[32,3]{0,1:T(4,128)S(1)}, s32[32,3]{0,1:T(4,128)}, u32[]{:S(2)}) copy-start(s32[32,3]{0,1:T(4,128)} %param.10) | copy-start | bytes 1156
  146.5 41.9 %all-to-all-start.3 = ((bf16[16,8,2560]{2,1,0:T(8,128)(2,1)}), bf16[16,8,2560]{2,1,0:T(8,128)(2,1)S(1)}, u32[]{:S(2)}, u32[]{:S(2)}) async-start(bf16[16,8,2560]{2,1,0:T(8,128)(2,1)} %bitcast.9), calls=%async_computation.3 | async-start | bytes 1310720 | tf_op jit(solution)/shard_map/all_to_all | solution.py:293

commit v5 on v4

--- a/solution.py
+++ b/solution.py
@@ -42,48 +42,22 @@
     return heres, held
 
 
-def stack_kernel(w_gate, w_up, w_down, stacked, held, in_sems, out_sems):
-    part = w_gate.shape[1] // 2
+def pack_kernel(
+    groups, picks, gates, tokens, w_up, w_down, packed, stacked, held_weights, in_sems, out_sems
+):
+    tok, width = tokens.shape
+    part = w_up.shape[1] // 2
     inward, outward = [], []
-    for i, weight in enumerate((w_gate, w_up, w_down)):
+    for i, weight in enumerate((w_up, w_down)):
         for j in range(2):
             block = pl.ds((2 * i + j) * part, part)
             source = weight.at[0, pl.ds(j * part, part)]
+            here = held_weights.at[block]
             sem = 2 * i + j
-            inward.append(pltpu.make_async_copy(source, held.at[block], in_sems.at[sem]))
-            outward.append(
-                pltpu.make_async_copy(held.at[block], stacked.at[block], out_sems.at[sem])
-            )
+            inward.append(pltpu.make_async_copy(source, here, in_sems.at[sem]))
+            outward.append(pltpu.make_async_copy(here, stacked.at[block], out_sems.at[sem]))
     for copy in inward:
         copy.start()
-    for arrival, copy in zip(inward, outward):
-        arrival.wait()
-        copy.start()
-    for copy in outward:
-        copy.wait()
-
-
-def stack(w_gate, w_up, w_down):
-    _, hidden, width = w_gate.shape
-    whole = (3 * hidden, width)
-    return pl.pallas_call(
-        stack_kernel,
-        out_shape=jax.ShapeDtypeStruct(whole, BF),
-        in_specs=[ANY] * 3,
-        out_specs=ANY,
-        scratch_shapes=[
-            pltpu.VMEM(whole, BF),
-            pltpu.SemaphoreType.DMA((6,)),
-            pltpu.SemaphoreType.DMA((6,)),
-        ],
-        compiler_params=pltpu.CompilerParams(vmem_limit_bytes=60 << 20),
-        name="stack",
-    )(w_gate, w_up, w_down)
-
-
-def pack_kernel(groups, picks, gates, tokens, *refs):
-    packed = refs[-1]
-    tok, width = tokens.shape
     heres, held = find_slots(groups, tok)
 
     def select(values, j):
@@ -94,6 +68,9 @@
 
     labels = picks[...].astype(F32) + 1.0
     probs = gates[...]
+    for arrival, copy in zip(inward, outward):
+        arrival.wait()
+        copy.start()
     lane = iota((HELD, META), 1)
     cols = jnp.zeros((HELD, META), F32)
     for j in range(2):
@@ -105,22 +82,30 @@
             cols = jnp.where(lane == place + j, value, cols)
     packed[:, width:] = cols.astype(BF)
     packed[:, :width] = jnp.dot(held.astype(BF), tokens[...], preferred_element_type=F32).astype(BF)
-
-
-def pack(tokens, groups, picks, gates, *after):
+    for copy in outward:
+        copy.wait()
+
+
+def pack(tokens, groups, picks, gates, w_up, w_down):
     tok, width = tokens.shape
     small = [groups.T, picks.T, gates.T, tokens]
     whole = lambda shape: pl.BlockSpec(shape, lambda i: (0,) * len(shape))
     out = jax.ShapeDtypeStruct((HELD, width + META), BF)
+    stacked = jax.ShapeDtypeStruct((2 * w_up.shape[1], width), BF)
     return pl.pallas_call(
         pack_kernel,
         grid=(1,),
-        out_shape=out,
-        in_specs=[whole(array.shape) for array in small] + [ANY] * len(after),
-        out_specs=whole(out.shape),
-        compiler_params=pltpu.CompilerParams(vmem_limit_bytes=56 << 20),
+        out_shape=(out, stacked),
+        in_specs=[whole(array.shape) for array in small] + [ANY] * 2,
+        out_specs=(whole(out.shape), ANY),
+        scratch_shapes=[
+            pltpu.VMEM(stacked.shape, BF),
+            pltpu.SemaphoreType.DMA((4,)),
+            pltpu.SemaphoreType.DMA((4,)),
+        ],
+        compiler_params=pltpu.CompilerParams(vmem_limit_bytes=60 << 20),
         name="pack",
-    )(*small, *after)
+    )(*small, w_up, w_down)
 
 
 def slots_kernel(groups, *refs):
@@ -214,11 +199,12 @@
     return (gate_part / (1.0 + jnp.exp(-gate_part)) * up_part).astype(BF)
 
 
-def expert_kernel(rows, w_gate, w_up, w_down, other, outs, gate, up, down, sems):
+def expert_kernel(rows, w_gate, w_up, w_down, other_gate, other, outs, gate, up, down, sems):
     own = w_gate.shape[1]
     copies = []
     for i, (weight, here) in enumerate(((w_gate, gate), (w_up, up), (w_down, down))):
-        sources = (weight.at[0], other.at[pl.ds(i * own, own)])
+        more = other.at[pl.ds((i - 1) * own, own)] if i else other_gate
+        sources = (weight.at[0], more)
         copies.append(
             [
                 pltpu.make_async_copy(source, here.at[pl.ds(j * own, own)], sems.at[2 * i + j])
@@ -241,13 +227,13 @@
     outs[...] = jnp.dot(hidden, down[...], preferred_element_type=F32).astype(BF)
 
 
-def experts(rows, w_gate, w_up, w_down, other):
+def experts(rows, w_gate, w_up, w_down, other_gate, other):
     width = rows.shape[1]
     hidden = 2 * w_gate.shape[1]
     return pl.pallas_call(
         expert_kernel,
         out_shape=jax.ShapeDtypeStruct(rows.shape, BF),
-        in_specs=[VMEM] + [ANY] * 4,
+        in_specs=[VMEM] + [ANY] * 5,
         out_specs=VMEM,
         scratch_shapes=[pltpu.VMEM((hidden, width), BF)] * 3 + [pltpu.SemaphoreType.DMA((6,))],
         compiler_params=pltpu.CompilerParams(vmem_limit_bytes=40 << 20),
@@ -257,7 +243,7 @@
             transcendentals=rows.shape[0] * hidden,
         ),
         name="experts",
-    )(rows, w_gate, w_up, w_down, other)
+    )(rows, w_gate, w_up, w_down, other_gate, other)
 
 
 def unpack_kernel(slot, home, result):
@@ -300,12 +286,12 @@
 
 
 def on_device(tokens, chosen_groups, local_picks, gate_probs, w_gate, w_up, w_down):
-    stacked = stack(w_gate, w_up, w_down)
-    packed = pack(tokens, chosen_groups, local_picks, gate_probs, stacked)
+    packed, stacked = pack(tokens, chosen_groups, local_picks, gate_probs, w_up, w_down)
     other = from_neighbour(stacked)
+    other_gate = from_neighbour(w_gate[0])
     arrived = lax.cond(lax.axis_index("z") < N_RG, along_z, lambda block: block, packed)
-    rows = in_plane(spread(arrived, other))
-    outs = experts(rows, w_gate, w_up, w_down, other)
+    rows = in_plane(spread(arrived, other_gate, other))
+    outs = experts(rows, w_gate, w_up, w_down, other_gate, other)
     mixed = combine(arrived, in_plane(outs))
     return unpack(slots(chosen_groups, mixed), along_z(mixed))
 

time: 190 us -> 190 us (level)
  starting transfers between devices: 10.8 us -> 13.4 us
  blocking collectives: 131 us -> 129 us
    ppermute x1 -> x2, starting transfers between devices: 2.36 us -> 7.28 us  [from_neighbour(): return lax.ppermute(block, ('h', 'v', 'c'), pairs)]
    all_to_all x1, starting transfers between devices: 8.48 us -> 6.15 us  [along_z(): return lax.all_to_all(rows, 'z', 0, 0, tiled=True).reshape(shape)]
    all_to_all x1, blocking collectives: 53.5 us -> 51.4 us  [along_z(): return lax.all_to_all(rows, 'z', 0, 0, tiled=True).reshape(shape)]
    pallas_call x2 -> x1, Pallas kernels: 4.61 us -> 3.63 us  [pack(): pl.pallas_call(pack_kernel, grid=(1,), out_shape=(out, stacked), in_specs...]
  transfers between devices with their start and end apart: 2 -> 3, of which waited for: 1 -> 1; matrix products, arithmetic and copies ran while one was open for 0% -> 0% of each run, Pallas kernels for 1% -> 0%
where the time goes in v5:
time: 190 us
  blocking collectives  129 us (68%)
  waiting for transfers between devices  33.2 us (17%)
  Pallas kernels  13.5 us (7%)
  starting transfers between devices  13.4 us (7%)
    all_to_all x2, blocking collectives, in_plane(): lax.all_to_all(rows, ('h', 'x', 'c'), 0, 0, tiled=True).reshape(shape)  78 us
    all_to_all x1, blocking collectives, along_z(): return lax.all_to_all(rows, 'z', 0, 0, tiled=True).reshape(shape)  51.4 us
    all_to_all x1, waiting for transfers between devices, along_z(): return lax.all_to_all(rows, 'z', 0, 0, tiled=True).reshape(shape)  33.2 us
    ppermute x2, starting transfers between devices, from_neighbour(): return lax.ppermute(block, ('h', 'v', 'c'), pairs)  7.28 us
    pallas_call x1, Pallas kernels, experts(): pl.pallas_call(expert_kernel, out_shape=jax.ShapeDtypeStruct(rows.shape,...  6.16 us
    all_to_all x1, starting transfers between devices, along_z(): return lax.all_to_all(rows, 'z', 0, 0, tiled=True).reshape(shape)  6.15 us
  transfers between devices with their start and end apart: 3, of which 1 were waited for; matrix products, arithmetic and copies ran while one was open for 0% of the time, Pallas kernels for 0%

profile of v5, /device:TPU:40, one launch (start us, length us, event | category | flops | bytes accessed | tf_op | source)
XLA Modules:
  0.0 189.7 jit_solution(7270872103849696060)
XLA Ops:
  0.0 3.6 %pack.1 = (bf16[128,2688]{1,0:T(8,128)(2,1)S(1)}, bf16[512,2560]{1,0:T(8,128)(2,1)}) custom-call(s32[3,32]{1,0:T(4,128)} %bitcast.17, s32[6,32]{1,0:T(8,128)} %bitcast.22, f32[6,32]{1,0:T(8,128)} %bitcast.23, bf16[32,2560]{1,0:T(8,128)(2,1)} %tokens.1, bf16[1,256,2560]{2,1,0:T(8,128)(2,1)} %w_up.3, bf16[1,256,2560]{2,1,0:T(8,128)(2,1)} %w_down.3), custom_call_target="tpu_custom_call" | custom-call | tf_op jit(solution)/shard_map/pack/pallas_call | solution.py:95
  3.6 2.4 %collective-permute-start.1 = (bf16[512,2560]{1,0:T(8,128)(2,1)}, bf16[512,2560]{1,0:T(8,128)(2,1)S(1)}, u32[]{:S(2)}, u32[]{:S(2)}) collective-permute-start(bf16[512,2560]{1,0:T(8,128)(2,1)} %get-tuple-element.13), channel_id=1, source_target_pairs={{0,24},{1,9},{8,0},{9,17},{16,8},{17,25},{24,16},{25,1},{2,26},{3,... | collective-permute-start | bytes 7864328 | tf_op jit(solution)/shard_map/ppermute | solution.py:273
  6.0 4.9 %collective-permute-start = (bf16[256,2560]{1,0:T(8,128)(2,1)}, bf16[256,2560]{1,0:T(8,128)(2,1)}, u32[]{:S(2)}, u32[]{:S(2)}) collective-permute-start(bf16[256,2560]{1,0:T(8,128)(2,1)} %bitcast.19), channel_id=1, source_target_pairs={{0,24},{1,9},{8,0},{9,17},{16,8},{17,25},{24,16},{25,1},{2,26},{3,... | collective-permute-start | bytes 3932168 | tf_op jit(solution)/shard_map/ppermute | solution.py:273
  10.9 51.4 %conditional.1 = (bf16[128,2688]{1,0:T(8,128)(2,1)S(1)}) conditional(s32[]{:T(128)} %convert_element_type.3, bf16[128,2688]{1,0:T(8,128)(2,1)S(1)} %get-tuple-element.12, bf16[128,2688]{1,0:T(8,128)(2,1)S(1)} %get-tuple-element.12), branch_computations={%region_0.0_spmd, %region_1.0_spmd} | conditional | bytes 2752520 | solution.py:292
  11.0 51.4 %all_to_all.19 = bf16[16,8,2688]{2,1,0:T(8,128)(2,1)S(1)} all-to-all(bf16[16,8,2688]{2,1,0:T(8,128)(2,1)S(1)} %copy.10), channel_id=1, replica_groups=mesh['z'=16,'h'=2,'v'=2,'x'=4,'c'=2] {'z'}, dimensions={0} | all-to-all | bytes 1376256 | tf_op jit(solution)/shard_map/cond/branch_1_fun/all_to_all | solution.py:279
  62.4 0.0 collective-permute-done.refs_0_.other_gate
  62.4 0.0 collective-permute-done.1.refs_1_.other
  62.4 0.8 spread.1
  63.2 0.0 copy-start
  63.2 0.0 copy-start.1
  63.2 0.0 copy-start.3
  63.2 40.5 %all_to_all.20 = bf16[16,32,2560]{2,1,0:T(8,128)(2,1)S(1)} all-to-all(bf16[16,32,2560]{2,1,0:T(8,128)(2,1)S(1)} %bitcast.12), channel_id=1, replica_groups=mesh['z'=16,'h'=2,'v'=2,'x'=4,'c'=2] {'h','x','c'}, dimensions={0} | all-to-all | bytes 5242880 | tf_op jit(solution)/shard_map/all_to_all | solution.py:285
  103.7 0.0 copy-done
  103.7 0.0 copy-done.1
  103.7 0.0 copy-done.3
  103.7 6.2 %experts.1 = bf16[512,2560]{1,0:T(8,128)(2,1)S(1)} custom-call(bf16[512,2560]{1,0:T(8,128)(2,1)S(1)} %bitcast.14, bf16[1,256,2560]{2,1,0:T(8,128)(2,1)S(1)} %copy-done.3, bf16[1,256,2560]{2,1,0:T(8,128)(2,1)S(1)} %copy-done, bf16[1,256,2560]{2,1,0:T(8,128)(2,1)S(1)} %copy-done.1, bf16[256,2560]{1,0:T(8,128)(2,1)} %collective-permute-done.refs_0_.other_gate, ...), custom_call_target="tpu_custom_call" | custom-call | flops 4026531840 | bytes 13107200 | tf_op jit(solution)/shard_map/experts/pallas_call | solution.py:233
  109.9 37.5 %all_to_all.21 = bf16[16,32,2560]{2,1,0:T(8,128)(2,1)S(1)} all-to-all(bf16[16,32,2560]{2,1,0:T(8,128)(2,1)S(1)} %bitcast.15), channel_id=1, replica_groups=mesh['z'=16,'h'=2,'v'=2,'x'=4,'c'=2] {'h','x','c'}, dimensions={0} | all-to-all | bytes 5242880 | tf_op jit(solution)/shard_map/all_to_all | solution.py:285
  147.3 0.0 copy-start.2
  147.3 1.9 %combine.1.refs_0_ = bf16[128,2560]{1,0:T(8,128)(2,1)} custom-call(bf16[128,2688]{1,0:T(8,128)(2,1)S(1)} %get-tuple-element.14.arrived.cols, bf16[512,2560]{1,0:T(8,128)(2,1)S(1)} %bitcast.13), custom_call_target="tpu_custom_call" | custom-call | flops 671088640 | bytes 3276800 | tf_op jit(solution)/shard_map/combine/pallas_call | solution.py:184
  149.2 6.1 %all-to-all-start.3 = ((bf16[16,8,2560]{2,1,0:T(8,128)(2,1)}), bf16[16,8,2560]{2,1,0:T(8,128)(2,1)S(1)}, u32[]{:S(2)}, u32[]{:S(2)}) async-start(bf16[16,8,2560]{2,1,0:T(8,128)(2,1)} %bitcast.10), calls=%async_computation.3 | async-start | bytes 1310720 | tf_op jit(solution)/shard_map/all_to_all | solution.py:279
  155.4 0.0 copy-done.2
  155.4 0.1 slots.1.slot
  155.5 33.2 %all-to-all-done.3 = bf16[16,8,2560]{2,1,0:T(8,128)(2,1)S(1)} async-done(((bf16[16,8,2560]{2,1,0:T(8,128)(2,1)}), bf16[16,8,2560]{2,1,0:T(8,128)(2,1)S(1)}, u32[]{:S(2)}, u32[]{:S(2)}) %all-to-all-start.3) | async-done | bytes 655392 | tf_op jit(solution)/shard_map/all_to_all | solution.py:279
  188.8 0.9 unpack.1
  (1 shorter events, 0.0 us)
Async XLA Ops:
  3.6 58.7 %collective-permute-start.1 = (bf16[512,2560]{1,0:T(8,128)(2,1)}, bf16[512,2560]{1,0:T(8,128)(2,1)S(1)}, u32[]{:S(2)}, u32[]{:S(2)}) collective-permute-start(bf16[512,2560]{1,0:T(8,128)(2,1)} %get-tuple-element.13), channel_id=1, source_target_pairs={{0,24},{1,9},{8,0},{9,17},{16,8},{17,25},{24,16},{25,1},{2,26},{3,... | collective-permute-start | bytes 7864328 | tf_op jit(solution)/shard_map/ppermute | solution.py:273
  6.0 56.4 %collective-permute-start = (bf16[256,2560]{1,0:T(8,128)(2,1)}, bf16[256,2560]{1,0:T(8,128)(2,1)}, u32[]{:S(2)}, u32[]{:S(2)}) collective-permute-start(bf16[256,2560]{1,0:T(8,128)(2,1)} %bitcast.19), channel_id=1, source_target_pairs={{0,24},{1,9},{8,0},{9,17},{16,8},{17,25},{24,16},{25,1},{2,26},{3,... | collective-permute-start | bytes 3932168 | tf_op jit(solution)/shard_map/ppermute | solution.py:273
  63.2 40.5 %copy-start = (bf16[1,256,2560]{2,1,0:T(8,128)(2,1)S(1)}, bf16[1,256,2560]{2,1,0:T(8,128)(2,1)}, u32[]{:S(2)}) copy-start(bf16[1,256,2560]{2,1,0:T(8,128)(2,1)} %w_up.3) | copy-start | bytes 3932164
  63.2 40.5 %copy-start.1 = (bf16[1,256,2560]{2,1,0:T(8,128)(2,1)S(1)}, bf16[1,256,2560]{2,1,0:T(8,128)(2,1)}, u32[]{:S(2)}) copy-start(bf16[1,256,2560]{2,1,0:T(8,128)(2,1)} %w_down.3) | copy-start | bytes 3932164
  63.2 40.5 %copy-start.3 = (bf16[1,256,2560]{2,1,0:T(8,128)(2,1)S(1)}, bf16[1,256,2560]{2,1,0:T(8,128)(2,1)}, u32[]{:S(2)}) copy-start(bf16[1,256,2560]{2,1,0:T(8,128)(2,1)} %w_gate.1) | copy-start | bytes 3932164
  147.3 8.1 %copy-start.2 = (s32[32,3]{0,1:T(4,128)S(1)}, s32[32,3]{0,1:T(4,128)}, u32[]{:S(2)}) copy-start(s32[32,3]{0,1:T(4,128)} %param.10) | copy-start | bytes 1156
  149.2 39.5 %all-to-all-start.3 = ((bf16[16,8,2560]{2,1,0:T(8,128)(2,1)}), bf16[16,8,2560]{2,1,0:T(8,128)(2,1)S(1)}, u32[]{:S(2)}, u32[]{:S(2)}) async-start(bf16[16,8,2560]{2,1,0:T(8,128)(2,1)} %bitcast.10), calls=%async_computation.3 | async-start | bytes 1310720 | tf_op jit(solution)/shard_map/all_to_all | solution.py:279

commit v6 on v4

--- a/solution.py
+++ b/solution.py
@@ -42,10 +42,10 @@
     return heres, held
 
 
-def stack_kernel(w_gate, w_up, w_down, stacked, held, in_sems, out_sems):
-    part = w_gate.shape[1] // 2
+def stack_kernel(w_up, w_down, stacked, held, in_sems, out_sems):
+    part = w_up.shape[1] // 2
     inward, outward = [], []
-    for i, weight in enumerate((w_gate, w_up, w_down)):
+    for i, weight in enumerate((w_up, w_down)):
         for j in range(2):
             block = pl.ds((2 * i + j) * part, part)
             source = weight.at[0, pl.ds(j * part, part)]
@@ -63,22 +63,22 @@
         copy.wait()
 
 
-def stack(w_gate, w_up, w_down):
-    _, hidden, width = w_gate.shape
-    whole = (3 * hidden, width)
+def stack(w_up, w_down):
+    _, hidden, width = w_up.shape
+    whole = (2 * hidden, width)
     return pl.pallas_call(
         stack_kernel,
         out_shape=jax.ShapeDtypeStruct(whole, BF),
-        in_specs=[ANY] * 3,
+        in_specs=[ANY] * 2,
         out_specs=ANY,
         scratch_shapes=[
             pltpu.VMEM(whole, BF),
-            pltpu.SemaphoreType.DMA((6,)),
-            pltpu.SemaphoreType.DMA((6,)),
+            pltpu.SemaphoreType.DMA((4,)),
+            pltpu.SemaphoreType.DMA((4,)),
         ],
         compiler_params=pltpu.CompilerParams(vmem_limit_bytes=60 << 20),
         name="stack",
-    )(w_gate, w_up, w_down)
+    )(w_up, w_down)
 
 
 def pack_kernel(groups, picks, gates, tokens, *refs):
@@ -214,11 +214,12 @@
     return (gate_part / (1.0 + jnp.exp(-gate_part)) * up_part).astype(BF)
 
 
-def expert_kernel(rows, w_gate, w_up, w_down, other, outs, gate, up, down, sems):
+def expert_kernel(rows, w_gate, w_up, w_down, other_gate, other, outs, gate, up, down, sems):
     own = w_gate.shape[1]
     copies = []
     for i, (weight, here) in enumerate(((w_gate, gate), (w_up, up), (w_down, down))):
-        sources = (weight.at[0], other.at[pl.ds(i * own, own)])
+        more = other.at[pl.ds((i - 1) * own, own)] if i else other_gate
+        sources = (weight.at[0], more)
         copies.append(
             [
                 pltpu.make_async_copy(source, here.at[pl.ds(j * own, own)], sems.at[2 * i + j])
@@ -241,13 +242,13 @@
     outs[...] = jnp.dot(hidden, down[...], preferred_element_type=F32).astype(BF)
 
 
-def experts(rows, w_gate, w_up, w_down, other):
+def experts(rows, w_gate, w_up, w_down, other_gate, other):
     width = rows.shape[1]
     hidden = 2 * w_gate.shape[1]
     return pl.pallas_call(
         expert_kernel,
         out_shape=jax.ShapeDtypeStruct(rows.shape, BF),
-        in_specs=[VMEM] + [ANY] * 4,
+        in_specs=[VMEM] + [ANY] * 5,
         out_specs=VMEM,
         scratch_shapes=[pltpu.VMEM((hidden, width), BF)] * 3 + [pltpu.SemaphoreType.DMA((6,))],
         compiler_params=pltpu.CompilerParams(vmem_limit_bytes=40 << 20),
@@ -257,7 +258,7 @@
             transcendentals=rows.shape[0] * hidden,
         ),
         name="experts",
-    )(rows, w_gate, w_up, w_down, other)
+    )(rows, w_gate, w_up, w_down, other_gate, other)
 
 
 def unpack_kernel(slot, home, result):
@@ -300,12 +301,13 @@
 
 
 def on_device(tokens, chosen_groups, local_picks, gate_probs, w_gate, w_up, w_down):
-    stacked = stack(w_gate, w_up, w_down)
+    stacked = stack(w_up, w_down)
     packed = pack(tokens, chosen_groups, local_picks, gate_probs, stacked)
     other = from_neighbour(stacked)
+    other_gate = from_neighbour(w_gate[0])
     arrived = lax.cond(lax.axis_index("z") < N_RG, along_z, lambda block: block, packed)
-    rows = in_plane(spread(arrived, other))
-    outs = experts(rows, w_gate, w_up, w_down, other)
+    rows = in_plane(spread(arrived, other_gate, other))
+    outs = experts(rows, w_gate, w_up, w_down, other_gate, other)
     mixed = combine(arrived, in_plane(outs))
     return unpack(slots(chosen_groups, mixed), along_z(mixed))
 

time: 190 us -> 189 us (level)
  the two profiles are of different devices: /device:TPU:40 before, /device:TPU:32 now
where the time goes in v6:
time: 189 us
  blocking collectives  130 us (69%)
  waiting for transfers between devices  33.2 us (18%)
  Pallas kernels  14 us (7%)
  starting transfers between devices  11.9 us (6%)
    all_to_all x2, blocking collectives, in_plane(): lax.all_to_all(rows, ('h', 'x', 'c'), 0, 0, tiled=True).reshape(shape)  78.4 us
    all_to_all x1, blocking collectives, along_z(): return lax.all_to_all(rows, 'z', 0, 0, tiled=True).reshape(shape)  51.3 us
    all_to_all x1, waiting for transfers between devices, along_z(): return lax.all_to_all(rows, 'z', 0, 0, tiled=True).reshape(shape)  33.2 us
    ppermute x2, starting transfers between devices, from_neighbour(): return lax.ppermute(block, ('h', 'v', 'c'), pairs)  7.58 us
    pallas_call x1, Pallas kernels, experts(): pl.pallas_call(expert_kernel, out_shape=jax.ShapeDtypeStruct(rows.shape,...  6.16 us
    all_to_all x1, starting transfers between devices, along_z(): return lax.all_to_all(rows, 'z', 0, 0, tiled=True).reshape(shape)  4.34 us
  transfers between devices with their start and end apart: 3, of which 1 were waited for; matrix products, arithmetic and copies ran while one was open for 0% of the time, Pallas kernels for 1%

profile of v6, /device:TPU:32, one launch (start us, length us, event | category | flops | bytes accessed | tf_op | source)
XLA Modules:
  0.0 189.1 jit_solution(5578096767351749756)
XLA Ops:
  0.0 2.7 %stack.1.refs_0_ = bf16[512,2560]{1,0:T(8,128)(2,1)} custom-call(bf16[1,256,2560]{2,1,0:T(8,128)(2,1)} %w_up.3, bf16[1,256,2560]{2,1,0:T(8,128)(2,1)} %w_down.3), custom_call_target="tpu_custom_call" | custom-call | tf_op jit(solution)/shard_map/stack/pallas_call | solution.py:69
  2.7 4.9 %collective-permute-start.1 = (bf16[512,2560]{1,0:T(8,128)(2,1)}, bf16[512,2560]{1,0:T(8,128)(2,1)S(1)}, u32[]{:S(2)}, u32[]{:S(2)}) collective-permute-start(bf16[512,2560]{1,0:T(8,128)(2,1)} %stack.1.refs_0_), channel_id=1, source_target_pairs={{0,24},{1,9},{8,0},{9,17},{16,8},{17,25},{24,16},{25,1},{2,26},{3,... | collective-permute-start | bytes 7864328 | tf_op jit(solution)/shard_map/ppermute | solution.py:288
  7.6 2.7 %collective-permute-start = (bf16[256,2560]{1,0:T(8,128)(2,1)}, bf16[256,2560]{1,0:T(8,128)(2,1)}, u32[]{:S(2)}, u32[]{:S(2)}) collective-permute-start(bf16[256,2560]{1,0:T(8,128)(2,1)} %bitcast.19), channel_id=1, source_target_pairs={{0,24},{1,9},{8,0},{9,17},{16,8},{17,25},{24,16},{25,1},{2,26},{3,... | collective-permute-start | bytes 3932168 | tf_op jit(solution)/shard_map/ppermute | solution.py:288
  10.3 1.4 pack.1
  11.7 51.4 %conditional.1 = (bf16[128,2688]{1,0:T(8,128)(2,1)S(1)}) conditional(s32[]{:T(128)} %convert_element_type.3, bf16[128,2688]{1,0:T(8,128)(2,1)S(1)} %pack.1, bf16[128,2688]{1,0:T(8,128)(2,1)S(1)} %pack.1), branch_computations={%region_0.0_spmd, %region_1.0_spmd} | conditional | bytes 2752520 | solution.py:308
  11.7 51.3 %all_to_all.19 = bf16[16,8,2688]{2,1,0:T(8,128)(2,1)S(1)} all-to-all(bf16[16,8,2688]{2,1,0:T(8,128)(2,1)S(1)} %copy.10), channel_id=1, replica_groups=mesh['z'=16,'h'=2,'v'=2,'x'=4,'c'=2] {'z'}, dimensions={0} | all-to-all | bytes 1376256 | tf_op jit(solution)/shard_map/cond/branch_1_fun/all_to_all | solution.py:294
  63.1 0.0 collective-permute-done.refs_0_.other_gate
  63.1 0.0 collective-permute-done.1.refs_1_.other
  63.1 0.8 spread.1
  63.9 0.0 copy-start
  63.9 0.0 copy-start.1
  63.9 0.0 copy-start.3
  63.9 40.9 %all_to_all.20 = bf16[16,32,2560]{2,1,0:T(8,128)(2,1)S(1)} all-to-all(bf16[16,32,2560]{2,1,0:T(8,128)(2,1)S(1)} %bitcast.12), channel_id=1, replica_groups=mesh['z'=16,'h'=2,'v'=2,'x'=4,'c'=2] {'h','x','c'}, dimensions={0} | all-to-all | bytes 5242880 | tf_op jit(solution)/shard_map/all_to_all | solution.py:300
  104.9 0.0 copy-done
  104.9 0.0 copy-done.1
  104.9 0.0 copy-done.3
  104.9 6.2 %experts.1 = bf16[512,2560]{1,0:T(8,128)(2,1)S(1)} custom-call(bf16[512,2560]{1,0:T(8,128)(2,1)S(1)} %bitcast.14, bf16[1,256,2560]{2,1,0:T(8,128)(2,1)S(1)} %copy-done.3, bf16[1,256,2560]{2,1,0:T(8,128)(2,1)S(1)} %copy-done, bf16[1,256,2560]{2,1,0:T(8,128)(2,1)S(1)} %copy-done.1, bf16[256,2560]{1,0:T(8,128)(2,1)} %collective-permute-done.refs_0_.other_gate, ...), custom_call_target="tpu_custom_call" | custom-call | flops 4026531840 | bytes 13107200 | tf_op jit(solution)/shard_map/experts/pallas_call | solution.py:248
  111.0 37.5 %all_to_all.21 = bf16[16,32,2560]{2,1,0:T(8,128)(2,1)S(1)} all-to-all(bf16[16,32,2560]{2,1,0:T(8,128)(2,1)S(1)} %bitcast.15), channel_id=1, replica_groups=mesh['z'=16,'h'=2,'v'=2,'x'=4,'c'=2] {'h','x','c'}, dimensions={0} | all-to-all | bytes 5242880 | tf_op jit(solution)/shard_map/all_to_all | solution.py:300
  148.5 0.0 copy-start.2
  148.5 1.9 %combine.1.refs_0_ = bf16[128,2560]{1,0:T(8,128)(2,1)} custom-call(bf16[128,2688]{1,0:T(8,128)(2,1)S(1)} %get-tuple-element.10.arrived.cols, bf16[512,2560]{1,0:T(8,128)(2,1)S(1)} %bitcast.13), custom_call_target="tpu_custom_call" | custom-call | flops 671088640 | bytes 3276800 | tf_op jit(solution)/shard_map/combine/pallas_call | solution.py:199
  150.4 4.3 %all-to-all-start.3 = ((bf16[16,8,2560]{2,1,0:T(8,128)(2,1)}), bf16[16,8,2560]{2,1,0:T(8,128)(2,1)S(1)}, u32[]{:S(2)}, u32[]{:S(2)}) async-start(bf16[16,8,2560]{2,1,0:T(8,128)(2,1)} %bitcast.10), calls=%async_computation.3 | async-start | bytes 1310720 | tf_op jit(solution)/shard_map/all_to_all | solution.py:294
  154.8 0.0 copy-done.2
  154.8 0.1 slots.1.slot
  154.9 33.2 %all-to-all-done.3 = bf16[16,8,2560]{2,1,0:T(8,128)(2,1)S(1)} async-done(((bf16[16,8,2560]{2,1,0:T(8,128)(2,1)}), bf16[16,8,2560]{2,1,0:T(8,128)(2,1)S(1)}, u32[]{:S(2)}, u32[]{:S(2)}) %all-to-all-start.3) | async-done | bytes 655392 | tf_op jit(solution)/shard_map/all_to_all | solution.py:294
  188.1 0.9 unpack.1
  (1 shorter events, 0.0 us)
Async XLA Ops:
  2.7 60.4 %collective-permute-start.1 = (bf16[512,2560]{1,0:T(8,128)(2,1)}, bf16[512,2560]{1,0:T(8,128)(2,1)S(1)}, u32[]{:S(2)}, u32[]{:S(2)}) collective-permute-start(bf16[512,2560]{1,0:T(8,128)(2,1)} %stack.1.refs_0_), channel_id=1, source_target_pairs={{0,24},{1,9},{8,0},{9,17},{16,8},{17,25},{24,16},{25,1},{2,26},{3,... | collective-permute-start | bytes 7864328 | tf_op jit(solution)/shard_map/ppermute | solution.py:288
  7.6 55.5 %collective-permute-start = (bf16[256,2560]{1,0:T(8,128)(2,1)}, bf16[256,2560]{1,0:T(8,128)(2,1)}, u32[]{:S(2)}, u32[]{:S(2)}) collective-permute-start(bf16[256,2560]{1,0:T(8,128)(2,1)} %bitcast.19), channel_id=1, source_target_pairs={{0,24},{1,9},{8,0},{9,17},{16,8},{17,25},{24,16},{25,1},{2,26},{3,... | collective-permute-start | bytes 3932168 | tf_op jit(solution)/shard_map/ppermute | solution.py:288
  63.9 41.0 %copy-start = (bf16[1,256,2560]{2,1,0:T(8,128)(2,1)S(1)}, bf16[1,256,2560]{2,1,0:T(8,128)(2,1)}, u32[]{:S(2)}) copy-start(bf16[1,256,2560]{2,1,0:T(8,128)(2,1)} %w_up.3) | copy-start | bytes 3932164
  63.9 41.0 %copy-start.1 = (bf16[1,256,2560]{2,1,0:T(8,128)(2,1)S(1)}, bf16[1,256,2560]{2,1,0:T(8,128)(2,1)}, u32[]{:S(2)}) copy-start(bf16[1,256,2560]{2,1,0:T(8,128)(2,1)} %w_down.3) | copy-start | bytes 3932164
  63.9 41.0 %copy-start.3 = (bf16[1,256,2560]{2,1,0:T(8,128)(2,1)S(1)}, bf16[1,256,2560]{2,1,0:T(8,128)(2,1)}, u32[]{:S(2)}) copy-start(bf16[1,256,2560]{2,1,0:T(8,128)(2,1)} %w_gate.1) | copy-start | bytes 3932164
  148.5 6.2 %copy-start.2 = (s32[32,3]{0,1:T(4,128)S(1)}, s32[32,3]{0,1:T(4,128)}, u32[]{:S(2)}) copy-start(s32[32,3]{0,1:T(4,128)} %param.10) | copy-start | bytes 1156
  150.4 37.7 %all-to-all-start.3 = ((bf16[16,8,2560]{2,1,0:T(8,128)(2,1)}), bf16[16,8,2560]{2,1,0:T(8,128)(2,1)S(1)}, u32[]{:S(2)}, u32[]{:S(2)}) async-start(bf16[16,8,2560]{2,1,0:T(8,128)(2,1)} %bitcast.10), calls=%async_computation.3 | async-start | bytes 1310720 | tf_op jit(solution)/shard_map/all_to_all | solution.py:294
